TPU v7x, 32 devices: a whole 2x2x4 slice. The times are simulated.
32 devices in a mesh: fsdp: 32 (over z, y, x, core).
Axes of the slice: x: 2, y: 2, z: 4, core: 2. Of those that a mesh axis runs over, the one named last changes fastest.
Arguments:
- tokens: bfloat16 [32768, 768], P('fsdp'), may hold values from -6 to 6
- lengths: int32 [64, 2], P('fsdp'), may hold values from 1 to 448, as said below
- gain_attn: bfloat16 [768], P('fsdp'), may hold values from 0.5 to 1.5
- w_query: bfloat16 [768, 768], P('fsdp'), may hold values from -0.0546875 to 0.0546875
- w_key: bfloat16 [768, 768], P('fsdp'), may hold values from -0.21875 to 0.21875
- w_value: bfloat16 [768, 768], P('fsdp'), may hold values from -0.21875 to 0.21875
- w_attn_out: bfloat16 [768, 768], P('fsdp'), may hold values from -0.875 to 0.875
- gain_ffn: bfloat16 [768], P('fsdp'), may hold values from 0.5 to 1.5
- w_ffn_in: bfloat16 [768, 3072], P('fsdp'), may hold values from -0.21875 to 0.21875
- w_ffn_out: bfloat16 [3072, 768], P('fsdp'), may hold values from -0.15625 to 0.15625
- bucket_bias_matrix: bfloat16 [32, 12], replicated, may hold values from -4 to 4
- cotangent: bfloat16 [32768, 768], P('fsdp'), may hold values from -6 to 6
Outputs:
- output: bfloat16 [32768, 768], P('fsdp')
- grad_tokens: bfloat16 [32768, 768], P('fsdp')
- grad_gain_attn: float32 [768], P('fsdp')
- grad_query: float32 [768, 768], P('fsdp')
- grad_key: float32 [768, 768], P('fsdp')
- grad_value: float32 [768, 768], P('fsdp')
- grad_attn_out: float32 [768, 768], P('fsdp')
- feedforward_gain_gradient: float32 [768], P('fsdp')
- grad_ffn_in: float32 [768, 3072], P('fsdp')
- grad_ffn_out: float32 [3072, 768], P('fsdp')
- grad_bias_table: float32 [32, 12], replicated
Inputs may be any that keep to these rules, and one draw needn't show every extreme that they name: Column 0 is the row's query length, 1 to 64; column 1 its passage length, 128 to 448; in every draw some row's two lengths add up to 512.
All inputs are finite; a program needn't handle non-finite values.
Results may differ from a plain program's by a relative error of at most 0.014.
Values may be sent and summed in bfloat16 or wider, within the bound.
No kernel may reach another device: no remote copies, remote signals or barrier semaphores. Data moves between devices by JAX's collectives and lax.ppermute only.
A program may use at most 192 MiB of HBM per device.

v0:
```python
import math

import jax
import jax.numpy as jnp
import numpy as np
from jax import lax
from jax.sharding import PartitionSpec as P

NB = 32
MAXD = 128
SEQ = 512


def bucket_ids(span_length):
    offset = np.arange(span_length)[None, :] - np.arange(span_length)[:, None]
    half_count = NB // 2
    exact_count = half_count // 2
    result = np.where(offset > 0, half_count, 0)
    distance = np.abs(offset)
    spread = exact_count + np.floor(
        np.log(np.maximum(distance, 1) / exact_count)
        / math.log(MAXD / exact_count)
        * (half_count - exact_count)
    )
    spread = np.minimum(spread, half_count - 1)
    result = result + np.where(distance < exact_count, distance, spread)
    return result.astype(np.int32)


def smooth_gate(values):
    return jax.nn.gelu(values, approximate=True)


def contract_rows(left, right):
    return lax.dot_general(
        left, right, (((0,), (0,)), ((), ())), preferred_element_type=jnp.float32
    )


def contract_cols(left, right):
    return lax.dot_general(
        left, right, (((1,), (1,)), ((), ())), preferred_element_type=jnp.float32
    )


def norm_scale(values):
    return lax.rsqrt(jnp.mean(values * values, axis=-1, keepdims=True) + 1e-06)


def rms_back(values, scale, gain, grad_normed):
    scaled = values * scale
    grad_gain = jnp.sum(grad_normed * scaled, axis=0)
    weighted = grad_normed * gain
    grad_values = scale * (weighted - scaled * jnp.mean(weighted * scaled, axis=-1, keepdims=True))
    return (grad_values, grad_gain)


def masked_scores(query_seq, key_seq, valid_len, bias_patch):
    scores = (
        jnp.einsum("qhd,khd->hqk", query_seq, key_seq, preferred_element_type=jnp.float32)
        + bias_patch
    )
    permitted_pairs = jnp.arange(scores.shape[-1]) < valid_len
    return jnp.where(permitted_pairs[None, None, :], scores, -1e30)


def per_device(
    tokens,
    lengths,
    gain_attn,
    w_query,
    w_key,
    w_value,
    w_attn_out,
    gain_ffn,
    w_ffn_in,
    w_ffn_out,
    bucket_bias_matrix,
    cotangent,
):
    seq_count = lengths.shape[0]
    slot_count = seq_count * SEQ
    heads = bucket_bias_matrix.shape[1]
    width = tokens.shape[1]
    head_size = width // heads
    valid = jnp.sum(lengths, axis=-1)
    factor = 1.0 / math.sqrt(slot_count * lax.axis_size("fsdp"))
    gathered = (
        lax.all_gather(gain_attn, "fsdp", axis=0, tiled=True),
        lax.all_gather(w_query, "fsdp", axis=0, tiled=True),
        lax.all_gather(w_key, "fsdp", axis=0, tiled=True),
        lax.all_gather(w_value, "fsdp", axis=0, tiled=True),
        lax.all_gather(w_attn_out, "fsdp", axis=0, tiled=True),
        lax.all_gather(gain_ffn, "fsdp", axis=0, tiled=True),
        lax.all_gather(w_ffn_in, "fsdp", axis=0, tiled=True),
        lax.all_gather(w_ffn_out, "fsdp", axis=0, tiled=True),
    )
    (
        full_gain_attn,
        full_query,
        full_key,
        full_value,
        full_attn_out,
        full_gain_ffn,
        full_ffn_in,
        full_ffn_out,
    ) = gathered
    bucket_flat = jnp.asarray(bucket_ids(SEQ)).reshape(-1)
    onehot_table = (
        jnp.arange(bucket_bias_matrix.shape[0], dtype=jnp.int32)[:, None] == bucket_flat[None, :]
    ).astype(jnp.bfloat16)
    bias_patch = contract_rows(bucket_bias_matrix, onehot_table).reshape(heads, SEQ, SEQ)
    inputs_f = tokens.astype(jnp.float32)
    grad_out = cotangent.astype(jnp.float32)
    scale_attn = norm_scale(inputs_f)
    normed_attn = (inputs_f * scale_attn * full_gain_attn.astype(jnp.float32)).astype(jnp.bfloat16)
    query_rows = jnp.dot(normed_attn, full_query, preferred_element_type=jnp.float32).astype(
        jnp.bfloat16
    )
    key_rows = jnp.dot(normed_attn, full_key, preferred_element_type=jnp.float32).astype(
        jnp.bfloat16
    )
    value_rows = jnp.dot(normed_attn, full_value, preferred_element_type=jnp.float32).astype(
        jnp.bfloat16
    )
    query_seqs = query_rows.reshape(seq_count, SEQ, heads, head_size)
    key_seqs = key_rows.reshape(seq_count, SEQ, heads, head_size)
    value_seqs = value_rows.reshape(seq_count, SEQ, heads, head_size)

    def forward_block(block_item):
        query_seq, key_seq, value_seq, valid_len = block_item
        scores = masked_scores(query_seq, key_seq, valid_len, bias_patch)
        row_peak = jnp.max(scores, axis=-1, keepdims=True)
        shifted_exp = jnp.exp(scores - row_peak)
        row_total = jnp.sum(shifted_exp, axis=-1, keepdims=True)
        attention_weights = (shifted_exp / row_total).astype(jnp.bfloat16)
        mixed_rows = jnp.einsum(
            "hqk,khd->qhd", attention_weights, value_seq, preferred_element_type=jnp.float32
        ).astype(jnp.bfloat16)
        return (mixed_rows, row_peak[..., 0] + jnp.log(row_total[..., 0]))

    mixed_seqs, log_totals = lax.map(forward_block, (query_seqs, key_seqs, value_seqs, valid))
    attended = mixed_seqs.reshape(slot_count, width)
    hidden = inputs_f + jnp.dot(attended, full_attn_out, preferred_element_type=jnp.float32)
    scale_ffn = norm_scale(hidden)
    normed_ffn = (hidden * scale_ffn * full_gain_ffn.astype(jnp.float32)).astype(jnp.bfloat16)
    pre_act = jnp.dot(normed_ffn, full_ffn_in, preferred_element_type=jnp.float32)
    activated_f, gate_pullback = jax.vjp(smooth_gate, pre_act)
    activated = activated_f.astype(jnp.bfloat16)
    output = (hidden + jnp.dot(activated, full_ffn_out, preferred_element_type=jnp.float32)).astype(
        jnp.bfloat16
    )
    regathered = (
        lax.all_gather(gain_attn, "fsdp", axis=0, tiled=True),
        lax.all_gather(w_query, "fsdp", axis=0, tiled=True),
        lax.all_gather(w_key, "fsdp", axis=0, tiled=True),
        lax.all_gather(w_value, "fsdp", axis=0, tiled=True),
        lax.all_gather(w_attn_out, "fsdp", axis=0, tiled=True),
        lax.all_gather(gain_ffn, "fsdp", axis=0, tiled=True),
        lax.all_gather(w_ffn_in, "fsdp", axis=0, tiled=True),
        lax.all_gather(w_ffn_out, "fsdp", axis=0, tiled=True),
    )
    (
        back_gain_attn,
        back_query,
        back_key,
        back_value,
        back_attn_out,
        back_gain_ffn,
        back_ffn_in,
        back_ffn_out,
    ) = regathered
    grad_ffn_out = contract_rows(activated, cotangent)
    grad_act = contract_cols(cotangent, back_ffn_out)
    grad_pre = gate_pullback(grad_act)[0].astype(jnp.bfloat16)
    grad_ffn_in = contract_rows(normed_ffn, grad_pre)
    grad_normed_ffn = contract_cols(grad_pre, back_ffn_in)
    grad_through_ffn, feedforward_gain_gradient = rms_back(
        hidden, scale_ffn, back_gain_ffn.astype(jnp.float32), grad_normed_ffn
    )
    grad_hidden = grad_out + grad_through_ffn
    grad_branch = grad_hidden.astype(jnp.bfloat16)
    grad_attn_out = contract_rows(attended, grad_branch)
    grad_attended = contract_cols(grad_branch, back_attn_out).astype(jnp.bfloat16)
    grad_mixed_seqs = grad_attended.reshape(seq_count, SEQ, heads, head_size)

    def backward_block(table_acc, block_item):
        query_seq, key_seq, value_seq, grad_mixed, log_total, valid_len = block_item
        scores = masked_scores(query_seq, key_seq, valid_len, bias_patch)
        attention_weights = jnp.exp(scores - log_total[..., None])
        grad_value_seq = jnp.einsum(
            "hqk,qhd->khd",
            attention_weights.astype(jnp.bfloat16),
            grad_mixed,
            preferred_element_type=jnp.float32,
        ).astype(jnp.bfloat16)
        grad_weights = jnp.einsum(
            "qhd,khd->hqk", grad_mixed, value_seq, preferred_element_type=jnp.float32
        )
        row_dot = jnp.sum(grad_weights * attention_weights, axis=-1, keepdims=True)
        grad_scores = (attention_weights * (grad_weights - row_dot)).astype(jnp.bfloat16)
        grad_query_seq = jnp.einsum(
            "hqk,khd->qhd", grad_scores, key_seq, preferred_element_type=jnp.float32
        ).astype(jnp.bfloat16)
        grad_key_seq = jnp.einsum(
            "hqk,qhd->khd", grad_scores, query_seq, preferred_element_type=jnp.float32
        ).astype(jnp.bfloat16)
        table_acc = table_acc + contract_cols(grad_scores.reshape(heads, SEQ * SEQ), onehot_table)
        return (table_acc, (grad_query_seq, grad_key_seq, grad_value_seq))

    table_start = jnp.zeros((heads, bucket_bias_matrix.shape[0]), jnp.float32)
    table_local, (grad_query_seqs, grad_key_seqs, grad_value_seqs) = lax.scan(
        backward_block,
        table_start,
        (query_seqs, key_seqs, value_seqs, grad_mixed_seqs, log_totals, valid),
    )
    grad_query_rows = grad_query_seqs.reshape(slot_count, width)
    grad_key_rows = grad_key_seqs.reshape(slot_count, width)
    grad_value_rows = grad_value_seqs.reshape(slot_count, width)
    grad_query = contract_rows(normed_attn, grad_query_rows)
    grad_key = contract_rows(normed_attn, grad_key_rows)
    grad_value = contract_rows(normed_attn, grad_value_rows)
    grad_normed_attn = (
        contract_cols(grad_query_rows, back_query)
        + contract_cols(grad_key_rows, back_key)
        + contract_cols(grad_value_rows, back_value)
    )
    grad_through_attn, grad_gain_attn = rms_back(
        inputs_f, scale_attn, back_gain_attn.astype(jnp.float32), grad_normed_attn
    )
    grad_tokens = (grad_hidden + grad_through_attn).astype(jnp.bfloat16)
    summed = (
        lax.psum_scatter(grad_gain_attn, "fsdp", scatter_dimension=0, tiled=True),
        lax.psum_scatter(grad_query, "fsdp", scatter_dimension=0, tiled=True),
        lax.psum_scatter(grad_key, "fsdp", scatter_dimension=0, tiled=True),
        lax.psum_scatter(grad_value, "fsdp", scatter_dimension=0, tiled=True),
        lax.psum_scatter(grad_attn_out, "fsdp", scatter_dimension=0, tiled=True),
        lax.psum_scatter(feedforward_gain_gradient, "fsdp", scatter_dimension=0, tiled=True),
        lax.psum_scatter(grad_ffn_in, "fsdp", scatter_dimension=0, tiled=True),
        lax.psum_scatter(grad_ffn_out, "fsdp", scatter_dimension=0, tiled=True),
    )
    table_total = lax.psum(table_local, "fsdp")
    scaled = tuple((item * factor for item in summed))
    return (
        output,
        grad_tokens,
        scaled[0],
        scaled[1],
        scaled[2],
        scaled[3],
        scaled[4],
        scaled[5],
        scaled[6],
        scaled[7],
        table_total.T * factor,
    )


def solution(mesh):
    placed = (
        P("fsdp", None),
        P("fsdp", None),
        P("fsdp"),
        P("fsdp", None),
        P("fsdp", None),
        P("fsdp", None),
        P("fsdp", None),
        P("fsdp"),
        P("fsdp", None),
        P("fsdp", None),
        P(),
        P("fsdp", None),
    )
    return jax.shard_map(
        per_device,
        mesh=mesh,
        in_specs=placed,
        out_specs=(
            P("fsdp", None),
            P("fsdp", None),
            P("fsdp"),
            P("fsdp", None),
            P("fsdp", None),
            P("fsdp", None),
            P("fsdp", None),
            P("fsdp"),
            P("fsdp", None),
            P("fsdp", None),
            P(),
        ),
        check_vma=False,
    )
```

profile of v0, /device:TPU:0, one launch (start us, length us, event | category | flops | bytes accessed | tf_op | source)
XLA Modules:
  0.0 1137.9 jit_solution(16744394071856747002)
XLA Ops:
  13.7 42.0 %all-reduce.5 = (bf16[768]{0:T(1024)(128)(2,1)S(1)}, bf16[768]{0:T(1024)(128)(2,1)S(1)}) all-reduce(bf16[768]{0:T(1024)(128)(2,1)S(1)} %dynamic-update-slice, bf16[768]{0:T(1024)(128)(2,1)S(1)} %dynamic-update-slice.1), channel_id=1, replica_groups=mesh['fsdp'=32] {'fsdp'}, use_global_device_ids=true, to_apply=%add | all-reduce | flops 1536 | bytes 6144
  67.0 19.1 %copy.121 = f32[2,8,512,512]{3,2,1,0:T(8,128)} copy(f32[2,8,512,512]{3,1,2,0:T(8,128)S(1)} %bitcast.178) | data formatting | bytes 33554432
  86.2 10.7 slice
  96.9 12.9 %copy.91 = f32[12,512,512]{1,2,0:T(8,128)} copy(f32[12,512,512]{2,1,0:T(8,128)} %slice) | data formatting | bytes 25165824 | tf_op jit(solution)/shard_map/while | solution.py:142
  133.4 46.1 %all-gather.7.cloned.1.call-done = bf16[768,768]{1,0:T(8,128)(2,1)} async-done(((bf16[24,768]{1,0:T(8,128)(2,1)}), bf16[768,768]{1,0:T(8,128)(2,1)}) %all-gather.7.cloned.1.call-update) | async-done | bytes 1179664 | tf_op jit(solution)/shard_map/all_gather | solution.py:92
  194.6 25.5 %while.29 = (s32[]{:T(128)}, bf16[2,512,12,64]{1,3,2,0:T(8,128)(2,1)}, f32[2,12,512]{2,1,0:T(8,128)S(1)}, bf16[2,512,12,64]{1,3,2,0:T(8,128)(2,1)}, s32[2]{0:T(1...) while((s32[]{:T(128)}, ...), condition=%wide.region_5.6_spmd, body=%wide.region_2.5_spmd.sunk | while | flops 830859776 | bytes 60009620 | solution.py:142
  224.7 10.6 all-gather.13.cloned.1.call-done
  240.7 59.9 %all-gather.15.cloned.1.call-done = bf16[768,3072]{1,0:T(8,128)(2,1)} async-done(((bf16[24,3072]{1,0:T(8,128)(2,1)}), bf16[768,3072]{1,0:T(8,128)(2,1)}) %all-gather.15.cloned.1.call-update) | async-done | bytes 4718608 | tf_op jit(solution)/shard_map/all_gather | solution.py:95
  300.6 11.0 fusion.82
  311.6 54.3 %all-gather.17.cloned.1.call-done = bf16[3072,768]{1,0:T(8,128)(2,1)} async-done(((bf16[96,768]{1,0:T(8,128)(2,1)}), bf16[3072,768]{1,0:T(8,128)(2,1)}) %all-gather.17.cloned.1.call-update) | async-done | bytes 4718608 | tf_op jit(solution)/shard_map/all_gather | solution.py:96
  365.9 17.3 %fusion.65 = bf16[1024,3072]{1,0:T(8,128)(2,1)} fusion(f32[1024,3072]{1,0:T(8,128)} %fusion.82, bf16[1024,768]{1,0:T(8,128)(2,1)} %param.28, bf16[3072,768]{1,0:T(8,128)(2,1)} %all-gather.17.cloned.1.call-done), kind=kOutput, calls=%fused_computation.71 | convolution fusion | flops 4894752768 | bytes 25165824 | tf_op jit(solution)/shard_map/dot_general | solution.py:41
  415.2 118.8 %while.30 = (s32[]{:T(128)}, f32[12,32]{1,0:T(8,128)S(1)}, bf16[2,512,12,64]{1,3,2,0:T(8,128)(2,1)}, bf16[2,512,12,64]{1,3,2,0:T(8,128)(2,1)}, bf16[2,512,12,64]...) while((s32[]{:T(128)}, f32[12,32]{1,0:T(8,128)S(1)}, ...), condition=%wide.region_10.11_spmd.clone, body=%wide.region_8.10_spmd.clone.sunk | while | flops 2260856064 | bytes 227157392 | solution.py:212
  440.7 8.7 copy.128
  456.1 11.8 %copy.129 = bf16[2,8,512,512]{3,1,2,0:T(8,128)(2,1)} copy(bf16[2,8,512,512]{3,2,1,0:T(8,128)(2,1)} %bitcast.176) | data formatting | bytes 16777216 | tf_op jit(solution)/shard_map/while
  500.0 8.7 copy.128
  515.4 11.5 %copy.129 = bf16[2,8,512,512]{3,1,2,0:T(8,128)(2,1)} copy(bf16[2,8,512,512]{3,2,1,0:T(8,128)(2,1)} %bitcast.176) | data formatting | bytes 16777216 | tf_op jit(solution)/shard_map/while
  555.7 12.9 %fusion.83 = f32[3072,768]{1,0:T(8,128)} fusion(bf16[1024,768]{1,0:T(8,128)(2,1)} %param.28, f32[1024,3072]{1,0:T(8,128)} %fusion.82), kind=kOutput, calls=%fused_computation.117 | convolution fusion | flops 4860149760 | bytes 23592960 | tf_op jit(solution)/shard_map/dot_general | solution.py:35
  569.4 10.6 fusion.81
  580.0 11.7 %add_convert_fusion = bf16[1024,768]{0,1:T(8,128)(2,1)} fusion(f32[1024,768]{0,1:T(8,128)} %get-tuple-element.327, bf16[3072,768]{1,0:T(8,128)(2,1)} %all-gather.17.cloned.1.call-done, f32[1024,3072]{1,0:T(8,128)} %fusion.82), kind=kOutput, calls=%fused_computation.92 | convolution fusion | flops 4861722624 | bytes 22020096 | tf_op jit(solution)/shard_map/dot_general | solution.py:150
  603.5 39.9 %all-reduce.4 = (f32[768]{0:T(1024)S(1)}, f32[768]{0:T(1024)S(1)}, f32[12,32]{1,0:T(8,128)S(1)}) all-reduce(f32[768]{0:T(1024)S(1)} %get-tuple-element.273, f32[768]{0:T(1024)S(1)} %copy-done.33, f32[12,32]{1,0:T(8,128)S(1)} %get-tuple-element.129), channel_id=2, replica_groups=mesh['fsdp'=32] {'fsdp'}, use_global_device_ids=true, to_apply=%region_13.14.clone | all-reduce | flops 1920 | bytes 15360
  647.6 95.3 %reduce-scatter.7.cloned.1.call-done = f32[24,768]{1,0:T(8,128)} async-done(((f32[768,768]{1,0:T(8,128)}), f32[24,768]{1,0:T(8,128)}) %reduce-scatter.7.cloned.1.call-update) | async-done | bytes 73744 | tf_op jit(solution)/shard_map/reduce_scatter | solution.py:234
  744.5 102.6 %reduce-scatter.11.cloned.1.call-done = f32[24,768]{1,0:T(8,128)} async-done(((f32[768,768]{1,0:T(8,128)}), f32[24,768]{1,0:T(8,128)}) %reduce-scatter.11.cloned.1.call-update) | async-done | bytes 73744 | tf_op jit(solution)/shard_map/reduce_scatter | solution.py:236
  848.6 139.0 %reduce-scatter.17.cloned.1.call-done = f32[96,768]{1,0:T(8,128)} async-done(((f32[3072,768]{1,0:T(8,128)}), f32[96,768]{1,0:T(8,128)}) %reduce-scatter.17.cloned.1.call-update) | async-done | bytes 294928 | tf_op jit(solution)/shard_map/reduce_scatter | solution.py:240
  989.2 139.8 %reduce-scatter.15.cloned.1.call-done = f32[24,3072]{1,0:T(8,128)} async-done(((f32[768,3072]{1,0:T(8,128)}), f32[24,3072]{1,0:T(8,128)}) %reduce-scatter.15.cloned.1.call-update) | async-done | bytes 294928 | tf_op jit(solution)/shard_map/reduce_scatter | solution.py:239
  (214 shorter events, 245.4 us)
Async XLA Ops:
  7.2 53.7 %copy-start = (bf16[32,12]{0,1:T(8,128)(2,1)S(1)}, bf16[32,12]{0,1:T(8,128)(2,1)}, u32[]{:S(2)}) copy-start(bf16[32,12]{0,1:T(8,128)(2,1)} %param.27) | copy-start | bytes 2308
  7.2 52.0 %copy-start.17 = (bf16[1024,768]{1,0:T(8,128)(2,1)S(1)}, bf16[1024,768]{1,0:T(8,128)(2,1)}, u32[]{:S(2)}) copy-start(bf16[1024,768]{1,0:T(8,128)(2,1)} %param.28) | copy-start | bytes 4718596
  7.2 102.6 %all-gather.11.cloned.1.call-start = ((), (), s32[]{:S(2)}) async-start(), calls=%async_computation.8 | async-start | bytes 1216512 | tf_op jit(solution)/shard_map/all_gather | solution.py:91
  7.9 115.7 %all-gather.9.cloned.1.call-start = ((), (), s32[]{:S(2)}) async-start(), calls=%async_computation.7 | async-start | bytes 1216512 | tf_op jit(solution)/shard_map/all_gather | solution.py:90
  8.7 170.8 %all-gather.7.cloned.1.call-start = ((), (), s32[]{:S(2)}) async-start(), calls=%async_computation.6 | async-start | bytes 1216512 | tf_op jit(solution)/shard_map/all_gather | solution.py:92
  9.4 225.8 %all-gather.13.cloned.1.call-start = ((), (), s32[]{:S(2)}) async-start(), calls=%async_computation.9 | async-start | bytes 1216512 | tf_op jit(solution)/shard_map/all_gather | solution.py:93
  10.0 290.6 %all-gather.15.cloned.1.call-start = ((), (), s32[]{:S(2)}) async-start(), calls=%async_computation.10 | async-start | bytes 4866048 | tf_op jit(solution)/shard_map/all_gather | solution.py:95
  10.6 355.3 %all-gather.17.cloned.1.call-start = ((), (), s32[]{:S(2)}) async-start(), calls=%async_computation.11 | async-start | bytes 4866048 | tf_op jit(solution)/shard_map/all_gather | solution.py:96
  11.2 633.4 %reduce-scatter.13.cloned.1.call-start = ((), (), s32[]{:S(2)}) async-start(), calls=%async_computation.15 | async-start | bytes 2433024 | tf_op jit(solution)/shard_map/reduce_scatter | solution.py:237
  55.8 123.7 %copy-start.28 = (f32[768]{0:T(1024)}, f32[768]{0:T(1024)S(1)}, u32[]{:S(2)}) copy-start(f32[768]{0:T(1024)S(1)} %convert_element_type.84) | copy-start | bytes 9220
  59.2 120.3 %copy-start.30 = (f32[1024]{0:T(1024)}, f32[1024]{0:T(1024)S(1)}, u32[]{:S(2)}) copy-start(f32[1024]{0:T(1024)S(1)} %add_rsqrt_fusion.1) | copy-start | bytes 12292
  96.9 13.0 %copy-start.9 = (bf16[1024,768]{0,1:T(8,128)(2,1)S(1)}, bf16[1024,768]{0,1:T(8,128)(2,1)}, u32[]{:S(2)}) copy-start(bf16[1024,768]{0,1:T(8,128)(2,1)} %copy-done.8) | copy-start | bytes 4718596
  235.3 65.4 %copy-start.24 = (f32[768]{0:T(1024)S(1)}, f32[768]{0:T(1024)}, u32[]{:S(2)}) copy-start(f32[768]{0:T(1024)} %convert_element_type.89) | copy-start | bytes 9220
  240.7 151.0 %copy-start.26 = (f32[1024]{0:T(1024)}, f32[1024]{0:T(1024)S(1)}, u32[]{:S(2)}) copy-start(f32[1024]{0:T(1024)S(1)} %add_rsqrt_fusion) | copy-start | bytes 12292
  365.9 17.3 %copy-start.14 = (f32[1024,768]{0,1:T(8,128)S(1)}, f32[1024,768]{0,1:T(8,128)}, u32[]{:S(2)}) copy-start(f32[1024,768]{0,1:T(8,128)} %get-tuple-element.327) | copy-start | bytes 9437188
  365.9 17.3 %copy-start.16 = (bf16[768,3072]{1,0:T(8,128)(2,1)S(1)}, bf16[768,3072]{1,0:T(8,128)(2,1)}, u32[]{:S(2)}) copy-start(bf16[768,3072]{1,0:T(8,128)(2,1)} %all-gather.15.cloned.1.call-done) | copy-start | bytes 14155780
  411.2 234.9 %reduce-scatter.9.cloned.1.call-start = ((), (), s32[]{:S(2)}) async-start(), calls=%async_computation.13 | async-start | bytes 2433024 | tf_op jit(solution)/shard_map/reduce_scatter | solution.py:235
  456.1 11.8 %copy-start.22 = (s32[262144]{0:T(1024)S(1)}, s32[262144]{0:T(1024)}, u32[]{:S(2)}) copy-start(s32[262144]{0:T(1024)} %get-tuple-element.539) | copy-start | bytes 3145732 | tf_op jit(solution)/shard_map/while
  515.4 11.5 %copy-start.22 = (s32[262144]{0:T(1024)S(1)}, s32[262144]{0:T(1024)}, u32[]{:S(2)}) copy-start(s32[262144]{0:T(1024)} %get-tuple-element.539) | copy-start | bytes 3145732 | tf_op jit(solution)/shard_map/while
  541.7 201.2 %reduce-scatter.7.cloned.1.call-start = ((), (), s32[]{:S(2)}) async-start(), calls=%async_computation.12 | async-start | bytes 2433024 | tf_op jit(solution)/shard_map/reduce_scatter | solution.py:234
  549.2 297.8 %reduce-scatter.11.cloned.1.call-start = ((), (), s32[]{:S(2)}) async-start(), calls=%async_computation.14 | async-start | bytes 2433024 | tf_op jit(solution)/shard_map/reduce_scatter | solution.py:236
  555.7 431.9 %reduce-scatter.17.cloned.1.call-start = ((), (), s32[]{:S(2)}) async-start(), calls=%async_computation.17 | async-start | bytes 9732096 | tf_op jit(solution)/shard_map/reduce_scatter | solution.py:240
  568.7 560.3 %reduce-scatter.15.cloned.1.call-start = ((), (), s32[]{:S(2)}) async-start(), calls=%async_computation.16 | async-start | bytes 9732096 | tf_op jit(solution)/shard_map/reduce_scatter | solution.py:239
  601.1 529.6 %copy-start.1 = (bf16[32,12]{0,1:T(8,128)(2,1)S(1)}, bf16[32,12]{0,1:T(8,128)(2,1)}, u32[]{:S(2)}) copy-start(bf16[32,12]{0,1:T(8,128)(2,1)} %param.27) | copy-start | bytes 2308
  (31 other events, 131.5 us)
Sparse Core Ops, SparseCore 0:
  10.9 56.7 all-gather.10
  70.7 52.8 all-gather.8
  126.5 52.9 all-gather.6
  182.3 52.9 all-gather.12
  238.0 62.5 all-gather.14
  303.4 62.4 all-gather.16
  411.3 97.8 reduce-scatter.12
  541.8 97.7 reduce-scatter.8
  644.9 97.9 reduce-scatter.6
  748.9 98.0 reduce-scatter.10
  852.9 134.5 reduce-scatter.16
  994.3 134.6 reduce-scatter.14
where the time goes:
time: 1150 us; the launch traced here: 1140 us
  waiting for transfers between devices  655 us (57%)
  matrix products  192 us (17%)
  local copies, waits for them, and re-layouts  165 us (14%)
  blocking collectives  81.9 us (7%)
  other arithmetic  27.6 us (2%)
  between operations  15 us (1%)
    reduce_scatter x1, waiting for transfers between devices, per_device(): lax.psum_scatter(grad_ffn_in, 'fsdp', scatter_dimension=0, tiled=True)  140 us
    reduce_scatter x1, waiting for transfers between devices, per_device(): lax.psum_scatter(grad_ffn_out, 'fsdp', scatter_dimension=0, tiled=True)  139 us
    reduce_scatter x1, waiting for transfers between devices, per_device(): lax.psum_scatter(grad_value, 'fsdp', scatter_dimension=0, tiled=True)  103 us
    reduce_scatter x1, waiting for transfers between devices, per_device(): lax.psum_scatter(grad_query, 'fsdp', scatter_dimension=0, tiled=True)  95.3 us
    unnamed x2, blocking collectives  81.9 us
    all_gather x1, waiting for transfers between devices, per_device(): lax.all_gather(w_ffn_in, 'fsdp', axis=0, tiled=True)  59.9 us
    all_gather x1, waiting for transfers between devices, per_device(): lax.all_gather(w_ffn_out, 'fsdp', axis=0, tiled=True)  54.3 us
    dot_general x8, matrix products, contract_cols(): lax.dot_general(left, right, (((1,), (1,)), ((), ())), preferred_element_...  51.5 us
  transfers between devices with their start and end apart: 12, of which 9 were waited for; matrix products, arithmetic and copies ran while one was open for 29% of the time, Pallas kernels for 0%

commit v1 on v0

--- a/solution.py
+++ b/solution.py
@@ -4,6 +4,8 @@
 import jax.numpy as jnp
 import numpy as np
 from jax import lax
+from jax.experimental import pallas as pl
+from jax.experimental.pallas import tpu as pltpu
 from jax.sharding import PartitionSpec as P
 
 NB = 32
@@ -62,6 +64,271 @@
     )
     permitted_pairs = jnp.arange(scores.shape[-1]) < valid_len
     return jnp.where(permitted_pairs[None, None, :], scores, -1e30)
+
+
+def flip(mask, count):
+    return [(i, i ^ mask) for i in range(count)]
+
+
+def swap(array, mask):
+    return lax.ppermute(array, "fsdp", flip(mask, lax.axis_size("fsdp")))
+
+
+def gather_chips(unit):
+    line = lax.axis_size("fsdp") // 8
+    half = line // 2
+    near = jnp.stack([unit] + [swap(unit, 8 * hop) for hop in range(1, line)])
+    over_x, over_y = swap(near, 2), swap(near, 4)
+    return (near, over_x, over_y, swap(over_y[:half], 2), swap(over_x[half:], 4))
+
+
+def chip_distances():
+    line = lax.axis_size("fsdp") // 8
+    half = line // 2
+    blocks = []
+    for part, (plane, first, last) in enumerate(
+        ((0, 0, line), (1, 0, line), (2, 0, line), (3, 0, half), (3, half, line))
+    ):
+        blocks += [(part, hop - first, 4 * hop + plane) for hop in range(first, last)]
+    return blocks
+
+
+def scatter_chips(send, keep):
+    line = keep.shape[1]
+    half = line // 2
+
+    def add(*terms):
+        return sum(term.astype(jnp.float32) for term in terms)
+
+    def low(value):
+        return value.astype(jnp.bfloat16)
+
+    both = low(add(keep, swap(send, 1)))
+    via_x, via_y = swap(both[3, :half], 2), swap(both[3, half:], 4)
+    x_low, y_high = swap(both[1, :half], 2), swap(both[2, half:], 4)
+    y_low = swap(low(add(both[2, :half], via_x)), 4)
+    x_high = swap(low(add(both[1, half:], via_y)), 2)
+    total = jnp.concatenate(
+        [low(add(both[0, :half], x_low, y_low)), low(add(both[0, half:], x_high, y_high))]
+    )
+    return add(total[0], *[swap(total[hop], 8 * hop) for hop in range(1, line)])
+
+
+def copy_blocks(moves, place, sources, out_shapes):
+    def kernel(place_ref, *refs):
+        ins, outs, sems = refs[: len(sources)], refs[len(sources) : -1], refs[-1]
+        copies = [
+            pltpu.make_async_copy(source, target, sems.at[index])
+            for index, (source, target) in enumerate(moves(place_ref[0], ins, outs))
+        ]
+        for copy in copies:
+            copy.start()
+        for copy in copies:
+            copy.wait()
+
+    return pl.pallas_call(
+        kernel,
+        out_shape=out_shapes,
+        in_specs=[pl.BlockSpec(memory_space=pltpu.SMEM)]
+        + [pl.BlockSpec(memory_space=pl.ANY)] * len(sources),
+        out_specs=[pl.BlockSpec(memory_space=pl.ANY)] * len(out_shapes),
+        scratch_shapes=[pltpu.SemaphoreType.DMA((lax.axis_size("fsdp"),))],
+    )(place, *sources)
+
+
+def both_cores(parts):
+    return parts + tuple(swap(part, 1) for part in parts)
+
+
+def chip_unit(shard, core):
+    half = shard.shape[1] // 2
+    mine = lax.dynamic_slice_in_dim(shard, core * half, half, 1)
+    other = swap(lax.dynamic_slice_in_dim(shard, (1 - core) * half, half, 1), 1)
+    return jnp.where(
+        core == 0, jnp.concatenate([mine, other], 0), jnp.concatenate([other, mine], 0)
+    )
+
+
+def place_halves(parts, place, rows):
+    parts = both_cores(parts)
+    count = len(parts) // 2
+    chips = lax.axis_size("fsdp") // 2
+
+    def moves(me, ins, outs):
+        chip, core = me // 2, me % 2
+        for side in range(2):
+            for part, index, distance in chip_distances():
+                start = pl.multiple_of((chip ^ distance) * rows, 16)
+                yield (
+                    ins[side * count + part].at[index],
+                    outs[0].at[core ^ side, pl.ds(start, rows), :],
+                )
+
+    shape = jax.ShapeDtypeStruct((2, chips * rows, parts[0].shape[-1]), jnp.bfloat16)
+    return copy_blocks(moves, place, parts, [shape])[0]
+
+
+def place_rows(parts, place, rows):
+    parts = both_cores(parts)
+    count = len(parts) // 2
+
+    def moves(me, ins, outs):
+        chip, core = me // 2, me % 2
+        for side in range(2):
+            for part, index, distance in chip_distances():
+                start = pl.multiple_of(((chip ^ distance) * 2 + (core ^ side)) * rows, 16)
+                yield (ins[side * count + part].at[index], outs[0].at[pl.ds(start, rows), :])
+
+    shape = jax.ShapeDtypeStruct(
+        (lax.axis_size("fsdp") * rows, parts[0].shape[-1]), jnp.bfloat16
+    )
+    return copy_blocks(moves, place, parts, [shape])[0]
+
+
+def split_halves(halves, place):
+    line = lax.axis_size("fsdp") // 8
+    rows = halves.shape[1] // (4 * line)
+
+    def moves(me, ins, outs):
+        chip, core = me // 2, me % 2
+        for side in range(2):
+            for plane in range(4):
+                for hop in range(line):
+                    start = pl.multiple_of((chip ^ (4 * hop + plane)) * rows, 16)
+                    yield (
+                        ins[0].at[core ^ side, pl.ds(start, rows), :],
+                        outs[side].at[plane, hop],
+                    )
+
+    shape = jax.ShapeDtypeStruct((4, line, rows, halves.shape[-1]), jnp.bfloat16)
+    keep, send = copy_blocks(moves, place, [halves], [shape, shape])
+    return send, keep
+
+
+def split_rows(array, place):
+    line = lax.axis_size("fsdp") // 8
+    rows = array.shape[0] // (8 * line)
+
+    def moves(me, ins, outs):
+        chip, core = me // 2, me % 2
+        for side in range(2):
+            for plane in range(4):
+                for hop in range(line):
+                    start = pl.multiple_of(
+                        ((chip ^ (4 * hop + plane)) * 2 + (core ^ side)) * rows, 16
+                    )
+                    yield (ins[0].at[pl.ds(start, rows), :], outs[side].at[plane, hop])
+
+    shape = jax.ShapeDtypeStruct((4, line, rows, array.shape[-1]), jnp.bfloat16)
+    keep, send = copy_blocks(moves, place, [array], [shape, shape])
+    return send, keep
+
+
+def own_rows(chip_sum, core):
+    rows = chip_sum.shape[0] // 2
+    mine = lax.dynamic_slice_in_dim(chip_sum, core * rows, rows, 0)
+    other = swap(lax.dynamic_slice_in_dim(chip_sum, (1 - core) * rows, rows, 0), 1)
+    return mine, other
+
+
+def join_columns(mine, other, core):
+    return jnp.where(
+        core == 0, jnp.concatenate([mine, other], 1), jnp.concatenate([other, mine], 1)
+    )
+
+
+def gather_by_chips(
+    gain_attn, w_query, w_key, w_value, w_attn_out, gain_ffn, w_ffn_in, w_ffn_out
+):
+    me = lax.axis_index("fsdp")
+    core = me % 2
+    place = me.astype(jnp.int32)[None]
+    gains = jnp.pad(jnp.stack([gain_attn, gain_ffn], 1), ((0, 0), (0, 126)))
+    other_gains = swap(gains, 1)
+    chip_gains = jnp.where(
+        core == 0,
+        jnp.concatenate([gains, other_gains], 0),
+        jnp.concatenate([other_gains, gains], 0),
+    )
+    unit_qkv = jnp.concatenate(
+        [chip_unit(w_query, core), chip_unit(w_key, core), chip_unit(w_value, core), chip_gains], 1
+    )
+    unit_in = jnp.concatenate([chip_unit(w_attn_out, core), chip_unit(w_ffn_in, core)], 1)
+    chip_rows = unit_qkv.shape[0]
+    halves_qkv = place_halves(gather_chips(unit_qkv), place, chip_rows)
+    halves_in = place_halves(gather_chips(unit_in), place, chip_rows)
+    full_ffn_out = place_rows(gather_chips(w_ffn_out), place, w_ffn_out.shape[0])
+    return halves_qkv, halves_in, full_ffn_out
+
+
+def halves_of(*arrays):
+    return jnp.stack(
+        [
+            jnp.concatenate(
+                [
+                    array[:, part * array.shape[1] // 2 : (part + 1) * array.shape[1] // 2]
+                    for array in arrays
+                ],
+                1,
+            )
+            for part in range(2)
+        ]
+    )
+
+
+def gather_plain(
+    gain_attn, w_query, w_key, w_value, w_attn_out, gain_ffn, w_ffn_in, w_ffn_out
+):
+    def full(shard):
+        return lax.all_gather(shard, "fsdp", axis=0, tiled=True)
+
+    gains = jnp.pad(jnp.stack([full(gain_attn), full(gain_ffn)], 1), ((0, 0), (0, 126)))
+    return (
+        halves_of(full(w_query), full(w_key), full(w_value), jnp.concatenate([gains, gains], 1)),
+        halves_of(full(w_attn_out), full(w_ffn_in)),
+        full(w_ffn_out),
+    )
+
+
+def sum_by_chips(half_attn, half_in, grad_out):
+    me = lax.axis_index("fsdp")
+    core = me % 2
+    place = me.astype(jnp.int32)[None]
+    side = half_attn.shape[-1] // 4
+    sum_out = scatter_chips(*split_rows(grad_out, place))
+    sum_in = scatter_chips(*split_halves(half_in, place))
+    sum_attn = scatter_chips(*split_halves(half_attn, place))
+    mine, other = own_rows(sum_attn, core)
+    sums = [
+        join_columns(
+            mine[:, part * side : (part + 1) * side], other[:, part * side : (part + 1) * side], core
+        )
+        for part in range(4)
+    ]
+    return sums + [join_columns(*own_rows(sum_in, core), core), sum_out]
+
+
+def sum_plain(half_attn, half_in, grad_out):
+    side = half_attn.shape[-1] // 4
+
+    def owned(array):
+        return lax.psum_scatter(
+            array.astype(jnp.float32), "fsdp", scatter_dimension=0, tiled=True
+        )
+
+    grads = [
+        jnp.concatenate([part[0], part[1]], 1)
+        for part in [half_attn[:, :, k * side : (k + 1) * side] for k in range(4)] + [half_in]
+    ]
+    return [owned(grad) for grad in grads + [grad_out]]
+
+
+def sum_everywhere(vector):
+    mask = 1
+    while mask < lax.axis_size("fsdp"):
+        vector = vector + swap(vector, mask)
+        mask *= 2
+    return vector
 
 
 def per_device(
@@ -85,26 +352,27 @@
     head_size = width // heads
     valid = jnp.sum(lengths, axis=-1)
     factor = 1.0 / math.sqrt(slot_count * lax.axis_size("fsdp"))
-    gathered = (
-        lax.all_gather(gain_attn, "fsdp", axis=0, tiled=True),
-        lax.all_gather(w_query, "fsdp", axis=0, tiled=True),
-        lax.all_gather(w_key, "fsdp", axis=0, tiled=True),
-        lax.all_gather(w_value, "fsdp", axis=0, tiled=True),
-        lax.all_gather(w_attn_out, "fsdp", axis=0, tiled=True),
-        lax.all_gather(gain_ffn, "fsdp", axis=0, tiled=True),
-        lax.all_gather(w_ffn_in, "fsdp", axis=0, tiled=True),
-        lax.all_gather(w_ffn_out, "fsdp", axis=0, tiled=True),
-    )
-    (
-        full_gain_attn,
-        full_query,
-        full_key,
-        full_value,
-        full_attn_out,
-        full_gain_ffn,
-        full_ffn_in,
-        full_ffn_out,
-    ) = gathered
+    me = lax.axis_index("fsdp")
+    side = width // 2
+    by_chips = 2 * gain_attn.shape[0] % 16 == 0
+    if by_chips:
+        halves_qkv, halves_in, full_ffn_out = gather_by_chips(
+            gain_attn, w_query, w_key, w_value, w_attn_out, gain_ffn, w_ffn_in, w_ffn_out
+        )
+    else:
+        halves_qkv, halves_in, full_ffn_out = gather_plain(
+            gain_attn, w_query, w_key, w_value, w_attn_out, gain_ffn, w_ffn_in, w_ffn_out
+        )
+
+    def whole(halves, first, last):
+        return jnp.concatenate([halves[0, :, first:last], halves[1, :, first:last]], 1)
+
+    full_query = whole(halves_qkv, 0, side)
+    full_key = whole(halves_qkv, side, 2 * side)
+    full_value = whole(halves_qkv, 2 * side, 3 * side)
+    full_gain_attn, full_gain_ffn = halves_qkv[0, :, 3 * side], halves_qkv[0, :, 3 * side + 1]
+    full_attn_out = whole(halves_in, 0, side)
+    full_ffn_in = whole(halves_in, side, halves_in.shape[-1])
     bucket_flat = jnp.asarray(bucket_ids(SEQ)).reshape(-1)
     onehot_table = (
         jnp.arange(bucket_bias_matrix.shape[0], dtype=jnp.int32)[:, None] == bucket_flat[None, :]
@@ -150,38 +418,18 @@
     output = (hidden + jnp.dot(activated, full_ffn_out, preferred_element_type=jnp.float32)).astype(
         jnp.bfloat16
     )
-    regathered = (
-        lax.all_gather(gain_attn, "fsdp", axis=0, tiled=True),
-        lax.all_gather(w_query, "fsdp", axis=0, tiled=True),
-        lax.all_gather(w_key, "fsdp", axis=0, tiled=True),
-        lax.all_gather(w_value, "fsdp", axis=0, tiled=True),
-        lax.all_gather(w_attn_out, "fsdp", axis=0, tiled=True),
-        lax.all_gather(gain_ffn, "fsdp", axis=0, tiled=True),
-        lax.all_gather(w_ffn_in, "fsdp", axis=0, tiled=True),
-        lax.all_gather(w_ffn_out, "fsdp", axis=0, tiled=True),
-    )
-    (
-        back_gain_attn,
-        back_query,
-        back_key,
-        back_value,
-        back_attn_out,
-        back_gain_ffn,
-        back_ffn_in,
-        back_ffn_out,
-    ) = regathered
     grad_ffn_out = contract_rows(activated, cotangent)
-    grad_act = contract_cols(cotangent, back_ffn_out)
+    grad_act = contract_cols(cotangent, full_ffn_out)
     grad_pre = gate_pullback(grad_act)[0].astype(jnp.bfloat16)
     grad_ffn_in = contract_rows(normed_ffn, grad_pre)
-    grad_normed_ffn = contract_cols(grad_pre, back_ffn_in)
+    grad_normed_ffn = contract_cols(grad_pre, full_ffn_in)
     grad_through_ffn, feedforward_gain_gradient = rms_back(
-        hidden, scale_ffn, back_gain_ffn.astype(jnp.float32), grad_normed_ffn
+        hidden, scale_ffn, full_gain_ffn.astype(jnp.float32), grad_normed_ffn
     )
     grad_hidden = grad_out + grad_through_ffn
     grad_branch = grad_hidden.astype(jnp.bfloat16)
     grad_attn_out = contract_rows(attended, grad_branch)
-    grad_attended = contract_cols(grad_branch, back_attn_out).astype(jnp.bfloat16)
+    grad_attended = contract_cols(grad_branch, full_attn_out).astype(jnp.bfloat16)
     grad_mixed_seqs = grad_attended.reshape(seq_count, SEQ, heads, head_size)
 
     def backward_block(table_acc, block_item):
@@ -221,38 +469,41 @@
     grad_key = contract_rows(normed_attn, grad_key_rows)
     grad_value = contract_rows(normed_attn, grad_value_rows)
     grad_normed_attn = (
-        contract_cols(grad_query_rows, back_query)
-        + contract_cols(grad_key_rows, back_key)
-        + contract_cols(grad_value_rows, back_value)
+        contract_cols(grad_query_rows, full_query)
+        + contract_cols(grad_key_rows, full_key)
+        + contract_cols(grad_value_rows, full_value)
     )
     grad_through_attn, grad_gain_attn = rms_back(
-        inputs_f, scale_attn, back_gain_attn.astype(jnp.float32), grad_normed_attn
+        inputs_f, scale_attn, full_gain_attn.astype(jnp.float32), grad_normed_attn
     )
     grad_tokens = (grad_hidden + grad_through_attn).astype(jnp.bfloat16)
-    summed = (
-        lax.psum_scatter(grad_gain_attn, "fsdp", scatter_dimension=0, tiled=True),
-        lax.psum_scatter(grad_query, "fsdp", scatter_dimension=0, tiled=True),
-        lax.psum_scatter(grad_key, "fsdp", scatter_dimension=0, tiled=True),
-        lax.psum_scatter(grad_value, "fsdp", scatter_dimension=0, tiled=True),
-        lax.psum_scatter(grad_attn_out, "fsdp", scatter_dimension=0, tiled=True),
-        lax.psum_scatter(feedforward_gain_gradient, "fsdp", scatter_dimension=0, tiled=True),
-        lax.psum_scatter(grad_ffn_in, "fsdp", scatter_dimension=0, tiled=True),
-        lax.psum_scatter(grad_ffn_out, "fsdp", scatter_dimension=0, tiled=True),
-    )
-    table_total = lax.psum(table_local, "fsdp")
-    scaled = tuple((item * factor for item in summed))
+    half_attn = halves_of(grad_query, grad_key, grad_value, grad_attn_out).astype(jnp.bfloat16)
+    half_in = halves_of(grad_ffn_in).astype(jnp.bfloat16)
+    sums = [
+        total * factor
+        for total in (sum_by_chips if by_chips else sum_plain)(
+            half_attn, half_in, grad_ffn_out.astype(jnp.bfloat16)
+        )
+    ]
+    small = sum_everywhere(
+        jnp.concatenate(
+            [grad_gain_attn, feedforward_gain_gradient, table_local.T.reshape(-1)]
+        ).reshape(-1, 128)
+    )
+    small = small.reshape(-1) * factor
+    shard = gain_attn.shape[0]
     return (
         output,
         grad_tokens,
-        scaled[0],
-        scaled[1],
-        scaled[2],
-        scaled[3],
-        scaled[4],
-        scaled[5],
-        scaled[6],
-        scaled[7],
-        table_total.T * factor,
+        lax.dynamic_slice_in_dim(small, me * shard, shard),
+        sums[0],
+        sums[1],
+        sums[2],
+        sums[3],
+        lax.dynamic_slice_in_dim(small, width + me * shard, shard),
+        sums[4],
+        sums[5],
+        small[2 * width :].reshape(bucket_bias_matrix.shape),
     )
 
 

time: 1150 us -> 1470 us (1.28)
  Pallas kernels: 0 us -> 878 us
  waiting for transfers between devices: 655 us -> 108 us
  blocking collectives: 81.9 us -> 0 us
  starting transfers between devices: 0.47 us -> 75.1 us
  local copies, waits for them, and re-layouts: 165 us -> 191 us
  matrix products: 192 us -> 168 us
  other arithmetic: 27.6 us -> 44.5 us
    pallas_call x0 -> x6, Pallas kernels: none -> 878 us  [copy_blocks(): pl.pallas_call(kernel, out_shape=out_shapes, in_specs=[pl.BlockSpec(memor...]
    reduce_scatter x6 -> x0, waiting for transfers between devices: 477 us -> none  [the longest x1 140 us: per_device(): lax.psum_scatter(grad_ffn_in, 'fsdp', scatter_dimension=0, tiled=True)]
    all_gather x6 -> x0, waiting for transfers between devices: 175 us -> none  [the longest x1 59.9 us: per_device(): lax.all_gather(w_ffn_in, 'fsdp', axis=0, tiled=True)]
    ppermute x0 -> x79, waiting for transfers between devices: none -> 108 us  [swap(): return lax.ppermute(array, 'fsdp', flip(mask, lax.axis_size('fsdp')))]
    unnamed x2 -> x0, blocking collectives: 81.9 us -> none
    ppermute x0 -> x79, starting transfers between devices: none -> 75.1 us  [swap(): return lax.ppermute(array, 'fsdp', flip(mask, lax.axis_size('fsdp')))]
    unnamed x68 -> x133, local copies, waits for them, and re-layouts: 39.4 us -> 40.1 us
  transfers between devices with their start and end apart: 12 -> 79, of which waited for: 9 -> 18; matrix products, arithmetic and copies ran while one was open for 29% -> 12% of each run, Pallas kernels for 0% -> 48%
where the time goes in v1:
time: 1470 us
  Pallas kernels  878 us (60%)
  local copies, waits for them, and re-layouts  191 us (13%)
  matrix products  168 us (11%)
  waiting for transfers between devices  108 us (7%)
  starting transfers between devices  75.1 us (5%)
  other arithmetic  44.5 us (3%)
    pallas_call x6, Pallas kernels, copy_blocks(): pl.pallas_call(kernel, out_shape=out_shapes, in_specs=[pl.BlockSpec(memor...  878 us
    ppermute x79, waiting for transfers between devices, swap(): return lax.ppermute(array, 'fsdp', flip(mask, lax.axis_size('fsdp')))  108 us
    ppermute x79, starting transfers between devices, swap(): return lax.ppermute(array, 'fsdp', flip(mask, lax.axis_size('fsdp')))  75.1 us
    dot_general x8, matrix products, contract_cols(): lax.dot_general(left, right, (((1,), (1,)), ((), ())), preferred_element_...  50.2 us
    unnamed x133, local copies, waits for them, and re-layouts  40.1 us
    while x36, local copies, waits for them, and re-layouts  36.7 us
    dot_general x7, matrix products, contract_rows(): lax.dot_general(left, right, (((0,), (0,)), ((), ())), preferred_element_...  33.8 us
  transfers between devices with their start and end apart: 79, of which 18 were waited for; matrix products, arithmetic and copies ran while one was open for 12% of the time, Pallas kernels for 48%

profile of v1, /device:TPU:0, one launch (start us, length us, event | category | flops | bytes accessed | tf_op | source)
XLA Modules:
  0.0 1467.7 jit_solution(7726360450976795635)
XLA Ops:
  45.1 9.7 collective-permute-done.19
  63.6 8.6 fusion.57
  81.1 17.8 %copy.150 = f32[2,8,512,512]{3,2,1,0:T(8,128)} copy(f32[2,8,512,512]{3,1,2,0:T(8,128)} %bitcast.349) | data formatting | bytes 33554432
  98.9 10.7 slice.376
  109.6 13.2 copy.108
  132.3 120.5 %shard_map.212 = bf16[2,768,1280]{2,1,0:T(8,128)(2,1)} custom-call(s32[1]{0:T(128)} %bitcast.7.place_ref, bf16[4,48,1280]{2,1,0:T(8,128)(2,1)} %copy-done.32, bf16[4,48,1280]{2,1,0:T(8,128)(2,1)} %copy-done.42, bf16[4,48,1280]{2,1,0:T(8,128)(2,1)} %copy-done.41, bf16[2,48,1280]{2,1,0:T(8,128)(2,1)} %copy-done.59, bf16[2,48,1280]{2,1,0:T(8,128)(2,1)} %copy-done.60, ...), custom_call_target="tpu_custom_call" | custom-call | tf_op jit(solution)/shard_map/pallas_call | solution.py:129
  293.9 25.2 %while.29 = (s32[]{:T(128)}, bf16[2,512,12,64]{1,3,2,0:T(8,128)(2,1)}, f32[2,12,512]{2,1,0:T(8,128)S(1)}, bf16[2,512,12,64]{1,3,2,0:T(8,128)(2,1)}, s32[2]{0:T(1...) while((s32[]{:T(128)}, ...), condition=%wide.region_5.6_spmd, body=%wide.region_2.5_spmd.sunk | while | flops 830859776 | bytes 60009620 | solution.py:410
  323.8 144.3 %shard_map.214 = bf16[3072,768]{1,0:T(8,128)(2,1)} custom-call(s32[1]{0:T(128)} %bitcast.7.place_ref, bf16[4,96,768]{2,1,0:T(8,128)(2,1)} %pad_maximum_fusion.18.refs_0_, bf16[4,96,768]{2,1,0:T(8,128)(2,1)} %collective-permute-done.33.refs_1_, bf16[4,96,768]{2,1,0:T(8,128)(2,1)} %collective-permute-done.34.refs_2_, ...), custom_call_target="tpu_custom_call" | custom-call | tf_op jit(solution)/shard_map/pallas_call | solution.py:129
  468.1 180.1 %shard_map.213 = bf16[2,768,1920]{2,1,0:T(8,128)(2,1)} custom-call(s32[1]{0:T(128)} %bitcast.7.place_ref, bf16[4,48,1920]{2,1,0:T(8,128)(2,1)} %pad_maximum_fusion.17.refs_0_, bf16[4,48,1920]{2,1,0:T(8,128)(2,1)} %collective-permute-done.21.refs_1_, bf16[4,48,1920]{2,1,0:T(8,128)(2,1)} %collective-permute-done.22.refs_2_, ...), custom_call_target="tpu_custom_call" | custom-call | tf_op jit(solution)/shard_map/pallas_call | solution.py:129
  662.0 10.3 add_convert_fusion.3
  672.3 14.9 %fusion.65 = bf16[1024,3072]{1,0:T(8,128)(2,1)} fusion(f32[1024,3072]{1,0:T(8,128)S(1)} %fusion.82, bf16[3072,768]{1,0:T(8,128)(2,1)} %shard_map.214, bf16[1024,768]{1,0:T(8,128)(2,1)S(1)} %copy-done.33), kind=kOutput, calls=%fused_computation.71 | convolution fusion | flops 4894752768 | bytes 25165824 | tf_op jit(solution)/shard_map/dot_general | solution.py:43
  687.2 9.4 convolution_convert_fusion.2.refs_0_
  696.7 9.0 multiply_reduce_fusion.1
  732.2 118.3 %while.30 = (s32[]{:T(128)}, f32[12,32]{1,0:T(8,128)S(1)}, bf16[2,512,12,64]{1,3,2,0:T(8,128)(2,1)}, bf16[2,512,12,64]{1,3,2,0:T(8,128)(2,1)}, bf16[2,512,12,64]...) while((s32[]{:T(128)}, f32[12,32]{1,0:T(8,128)S(1)}, ...), condition=%wide.region_10.11_spmd.clone, body=%wide.region_8.10_spmd.clone.sunk | while | flops 2260856064 | bytes 227157392 | solution.py:460
  772.7 11.6 copy.158
  816.1 8.6 copy.157
  831.5 11.6 copy.158
  884.1 144.3 %shard_map.215 = (bf16[4,4,48,1536]{3,2,1,0:T(8,128)(2,1)}, bf16[4,4,48,1536]{3,2,1,0:T(8,128)(2,1)}) custom-call(s32[1]{0:T(128)} %bitcast.7.place_ref, bf16[2,768,1536]{2,1,0:T(8,128)(2,1)} %pad_maximum_fusion.1.refs_0_), custom_call_target="tpu_custom_call" | custom-call | tf_op jit(solution)/shard_map/pallas_call | solution.py:129
  1035.3 144.3 %shard_map.217 = (bf16[4,4,96,768]{3,2,1,0:T(8,128)(2,1)}, bf16[4,4,96,768]{3,2,1,0:T(8,128)(2,1)}) custom-call(s32[1]{0:T(128)} %bitcast.7.place_ref, bf16[3072,768]{1,0:T(8,128)(2,1)} %convolution_convert_fusion.2.refs_0_), custom_call_target="tpu_custom_call" | custom-call | tf_op jit(solution)/shard_map/pallas_call | solution.py:129
  1187.5 144.3 %shard_map.216 = (bf16[4,4,48,1536]{3,2,1,0:T(8,128)(2,1)}, bf16[4,4,48,1536]{3,2,1,0:T(8,128)(2,1)}) custom-call(s32[1]{0:T(128)} %bitcast.7.place_ref, bf16[2,768,1536]{2,1,0:T(8,128)(2,1)} %pad_maximum_fusion.2.refs_0_), custom_call_target="tpu_custom_call" | custom-call | tf_op jit(solution)/shard_map/pallas_call | solution.py:129
  1362.6 10.4 collective-permute-done.60
  1397.9 10.3 collective-permute-done.74
  1437.4 12.3 collective-permute-done.55
  1453.7 10.2 collective-permute-done.66
  (475 shorter events, 408.1 us)
Async XLA Ops:
  55.9 73.8 %collective-permute-start.11 = (bf16[4,48,1280]{2,1,0:T(8,128)(2,1)S(1)}, bf16[4,48,1280]{2,1,0:T(8,128)(2,1)S(1)}, u32[]{:S(2)}, u32[]{:S(2)}) collective-permute-start(bf16[4,48,1280]{2,1,0:T(8,128)(2,1)S(1)} %pad_maximum_fusion.19.refs_0_), channel_id=1, source_target_pairs={{0,1},{1,0},{2,3},{3,2},{4,5},{5,4},{6,7},{7,6},{8,9},{9,8},{10,11... | collective-permute-start | bytes 1474568 | tf_op jit(solution)/shard_map/ppermute | solution.py:74
  61.0 70.8 %collective-permute-start.13 = (bf16[4,48,1280]{2,1,0:T(8,128)(2,1)S(1)}, bf16[4,48,1280]{2,1,0:T(8,128)(2,1)}, u32[]{:S(2)}, u32[]{:S(2)}) collective-permute-start(bf16[4,48,1280]{2,1,0:T(8,128)(2,1)S(1)} %collective-permute-done.8.refs_2_), channel_id=1, source_target_pairs={{0,1},{1,0},{2,3},{3,2},{4,5},{5,4},{6,7},{7,6},{8,9},{9,8},{10,11... | collective-permute-start | bytes 1474568 | tf_op jit(solution)/shard_map/ppermute | solution.py:74
  62.9 68.9 %collective-permute-start.12 = (bf16[4,48,1280]{2,1,0:T(8,128)(2,1)S(1)}, bf16[4,48,1280]{2,1,0:T(8,128)(2,1)}, u32[]{:S(2)}, u32[]{:S(2)}) collective-permute-start(bf16[4,48,1280]{2,1,0:T(8,128)(2,1)S(1)} %collective-permute-done.7.refs_1_), channel_id=1, source_target_pairs={{0,1},{1,0},{2,3},{3,2},{4,5},{5,4},{6,7},{7,6},{8,9},{9,8},{10,11... | collective-permute-start | bytes 1474568 | tf_op jit(solution)/shard_map/ppermute | solution.py:74
  77.5 52.2 %collective-permute-start.14 = (bf16[2,48,1280]{2,1,0:T(8,128)(2,1)}, bf16[2,48,1280]{2,1,0:T(8,128)(2,1)}, u32[]{:S(2)}, u32[]{:S(2)}) collective-permute-start(bf16[2,48,1280]{2,1,0:T(8,128)(2,1)} %copy-done.59), channel_id=1, source_target_pairs={{0,1},{1,0},{2,3},{3,2},{4,5},{5,4},{6,7},{7,6},{8,9},{9,8},{10,11... | collective-permute-start | bytes 737288 | tf_op jit(solution)/shard_map/ppermute | solution.py:74
  77.5 53.8 %collective-permute-start.15 = (bf16[2,48,1280]{2,1,0:T(8,128)(2,1)}, bf16[2,48,1280]{2,1,0:T(8,128)(2,1)}, u32[]{:S(2)}, u32[]{:S(2)}) collective-permute-start(bf16[2,48,1280]{2,1,0:T(8,128)(2,1)} %copy-done.60), channel_id=1, source_target_pairs={{0,1},{1,0},{2,3},{3,2},{4,5},{5,4},{6,7},{7,6},{8,9},{9,8},{10,11... | collective-permute-start | bytes 737288 | tf_op jit(solution)/shard_map/ppermute | solution.py:74
  129.7 147.0 %collective-permute-start.37 = (bf16[4,96,768]{2,1,0:T(8,128)(2,1)}, bf16[4,96,768]{2,1,0:T(8,128)(2,1)}, u32[]{:S(2)}, u32[]{:S(2)}) collective-permute-start(bf16[4,96,768]{2,1,0:T(8,128)(2,1)} %pad_maximum_fusion.18.refs_0_), channel_id=1, source_target_pairs={{0,1},{1,0},{2,3},{3,2},{4,5},{5,4},{6,7},{7,6},{8,9},{9,8},{10,11... | collective-permute-start | bytes 1769480 | tf_op jit(solution)/shard_map/ppermute | solution.py:74
  129.7 147.6 %collective-permute-start.35 = (bf16[2,96,768]{2,1,0:T(8,128)(2,1)}, bf16[2,96,768]{2,1,0:T(8,128)(2,1)}, u32[]{:S(2)}, u32[]{:S(2)}) collective-permute-start(bf16[2,96,768]{2,1,0:T(8,128)(2,1)} %slice.323), channel_id=1, source_target_pairs={{0,2},{1,3},{2,0},{3,1},{4,6},{5,7},{6,4},{7,5},{8,10},{9,11},{10,... | collective-permute-start | bytes 884744 | tf_op jit(solution)/shard_map/ppermute | solution.py:74
  131.3 147.5 %collective-permute-start.36 = (bf16[2,96,768]{2,1,0:T(8,128)(2,1)}, bf16[2,96,768]{2,1,0:T(8,128)(2,1)}, u32[]{:S(2)}, u32[]{:S(2)}) collective-permute-start(bf16[2,96,768]{2,1,0:T(8,128)(2,1)} %slice.324), channel_id=1, source_target_pairs={{0,4},{1,5},{2,6},{3,7},{4,0},{5,1},{6,2},{7,3},{8,12},{9,13},{10,... | collective-permute-start | bytes 884744 | tf_op jit(solution)/shard_map/ppermute | solution.py:74
  131.8 147.0 %collective-permute-start.39 = (bf16[4,96,768]{2,1,0:T(8,128)(2,1)}, bf16[4,96,768]{2,1,0:T(8,128)(2,1)}, u32[]{:S(2)}, u32[]{:S(2)}) collective-permute-start(bf16[4,96,768]{2,1,0:T(8,128)(2,1)} %collective-permute-done.34.refs_2_), channel_id=1, source_target_pairs={{0,1},{1,0},{2,3},{3,2},{4,5},{5,4},{6,7},{7,6},{8,9},{9,8},{10,11... | collective-permute-start | bytes 1769480 | tf_op jit(solution)/shard_map/ppermute | solution.py:74
  131.8 159.7 %collective-permute-start.38 = (bf16[4,96,768]{2,1,0:T(8,128)(2,1)}, bf16[4,96,768]{2,1,0:T(8,128)(2,1)}, u32[]{:S(2)}, u32[]{:S(2)}) collective-permute-start(bf16[4,96,768]{2,1,0:T(8,128)(2,1)} %collective-permute-done.33.refs_1_), channel_id=1, source_target_pairs={{0,1},{1,0},{2,3},{3,2},{4,5},{5,4},{6,7},{7,6},{8,9},{9,8},{10,11... | collective-permute-start | bytes 1769480 | tf_op jit(solution)/shard_map/ppermute | solution.py:74
  291.5 176.6 %collective-permute-start.25 = (bf16[4,48,1920]{2,1,0:T(8,128)(2,1)}, bf16[4,48,1920]{2,1,0:T(8,128)(2,1)}, u32[]{:S(2)}, u32[]{:S(2)}) collective-permute-start(bf16[4,48,1920]{2,1,0:T(8,128)(2,1)} %pad_maximum_fusion.17.refs_0_), channel_id=1, source_target_pairs={{0,1},{1,0},{2,3},{3,2},{4,5},{5,4},{6,7},{7,6},{8,9},{9,8},{10,11... | collective-permute-start | bytes 2211848 | tf_op jit(solution)/shard_map/ppermute | solution.py:74
  291.6 176.6 %collective-permute-start.27 = (bf16[4,48,1920]{2,1,0:T(8,128)(2,1)}, bf16[4,48,1920]{2,1,0:T(8,128)(2,1)}, u32[]{:S(2)}, u32[]{:S(2)}) collective-permute-start(bf16[4,48,1920]{2,1,0:T(8,128)(2,1)} %collective-permute-done.22.refs_2_), channel_id=1, source_target_pairs={{0,1},{1,0},{2,3},{3,2},{4,5},{5,4},{6,7},{7,6},{8,9},{9,8},{10,11... | collective-permute-start | bytes 2211848 | tf_op jit(solution)/shard_map/ppermute | solution.py:74
  292.0 176.1 %collective-permute-start.26 = (bf16[4,48,1920]{2,1,0:T(8,128)(2,1)}, bf16[4,48,1920]{2,1,0:T(8,128)(2,1)}, u32[]{:S(2)}, u32[]{:S(2)}) collective-permute-start(bf16[4,48,1920]{2,1,0:T(8,128)(2,1)} %collective-permute-done.21.refs_1_), channel_id=1, source_target_pairs={{0,1},{1,0},{2,3},{3,2},{4,5},{5,4},{6,7},{7,6},{8,9},{9,8},{10,11... | collective-permute-start | bytes 2211848 | tf_op jit(solution)/shard_map/ppermute | solution.py:74
  292.1 176.0 %collective-permute-start.28 = (bf16[2,48,1920]{2,1,0:T(8,128)(2,1)}, bf16[2,48,1920]{2,1,0:T(8,128)(2,1)}, u32[]{:S(2)}, u32[]{:S(2)}) collective-permute-start(bf16[2,48,1920]{2,1,0:T(8,128)(2,1)} %collective-permute-done.23.refs_3_), channel_id=1, source_target_pairs={{0,1},{1,0},{2,3},{3,2},{4,5},{5,4},{6,7},{7,6},{8,9},{9,8},{10,11... | collective-permute-start | bytes 1105928 | tf_op jit(solution)/shard_map/ppermute | solution.py:74
  292.5 175.6 %collective-permute-start.29 = (bf16[2,48,1920]{2,1,0:T(8,128)(2,1)}, bf16[2,48,1920]{2,1,0:T(8,128)(2,1)}, u32[]{:S(2)}, u32[]{:S(2)}) collective-permute-start(bf16[2,48,1920]{2,1,0:T(8,128)(2,1)} %collective-permute-done.24.refs_4_), channel_id=1, source_target_pairs={{0,1},{1,0},{2,3},{3,2},{4,5},{5,4},{6,7},{7,6},{8,9},{9,8},{10,11... | collective-permute-start | bytes 1105928 | tf_op jit(solution)/shard_map/ppermute | solution.py:74
  880.2 148.7 %collective-permute-start.42 = (f32[15,128]{1,0:T(8,128)S(1)}, f32[15,128]{1,0:T(8,128)S(1)}, u32[]{:S(2)}, u32[]{:S(2)}) collective-permute-start(f32[15,128]{1,0:T(8,128)S(1)} %maximum_bitcast_fusion.2), channel_id=1, source_target_pairs={{0,1},{1,0},{2,3},{3,2},{4,5},{5,4},{6,7},{7,6},{8,9},{9,8},{10,11... | collective-permute-start | bytes 23048 | tf_op jit(solution)/shard_map/ppermute | solution.py:74
  1028.4 313.2 %collective-permute-start.47 = (bf16[4,4,48,1536]{3,2,1,0:T(8,128)(2,1)}, bf16[4,4,48,1536]{3,2,1,0:T(8,128)(2,1)}, u32[]{:S(2)}, u32[]{:S(2)}) collective-permute-start(bf16[4,4,48,1536]{3,2,1,0:T(8,128)(2,1)} %get-tuple-element.137), channel_id=1, source_target_pairs={{0,1},{1,0},{2,3},{3,2},{4,5},{5,4},{6,7},{7,6},{8,9},{9,8},{10,11... | collective-permute-start | bytes 7077896 | tf_op jit(solution)/shard_map/ppermute | solution.py:74
  1028.9 150.8 %collective-permute-start.43 = (f32[15,128]{1,0:T(8,128)S(1)}, f32[15,128]{1,0:T(8,128)S(1)}, u32[]{:S(2)}, u32[]{:S(2)}) collective-permute-start(f32[15,128]{1,0:T(8,128)S(1)} %fusion.161), channel_id=1, source_target_pairs={{0,2},{1,3},{2,0},{3,1},{4,6},{5,7},{6,4},{7,5},{8,10},{9,11},{10,... | collective-permute-start | bytes 23048 | tf_op jit(solution)/shard_map/ppermute | solution.py:74
  1179.7 168.7 %collective-permute-start.69 = (bf16[4,4,96,768]{3,2,1,0:T(8,128)(2,1)}, bf16[4,4,96,768]{3,2,1,0:T(8,128)(2,1)}, u32[]{:S(2)}, u32[]{:S(2)}) collective-permute-start(bf16[4,4,96,768]{3,2,1,0:T(8,128)(2,1)} %get-tuple-element.141), channel_id=1, source_target_pairs={{0,1},{1,0},{2,3},{3,2},{4,5},{5,4},{6,7},{7,6},{8,9},{9,8},{10,11... | collective-permute-start | bytes 7077896 | tf_op jit(solution)/shard_map/ppermute | solution.py:74
  1185.4 146.5 %collective-permute-start.45 = (f32[15,128]{1,0:T(8,128)S(1)}, f32[15,128]{1,0:T(8,128)S(1)}, u32[]{:S(2)}, u32[]{:S(2)}) collective-permute-start(f32[15,128]{1,0:T(8,128)S(1)} %add.235), channel_id=1, source_target_pairs={{0,8},{1,9},{2,10},{3,11},{4,12},{5,13},{6,14},{7,15},{8,0},{9,1},... | collective-permute-start | bytes 23048 | tf_op jit(solution)/shard_map/ppermute | solution.py:74
  1344.9 30.4 %collective-permute-start.48 = (bf16[2,48,1536]{2,1,0:T(8,128)(2,1)S(1)}, bf16[2,48,1536]{2,1,0:T(8,128)(2,1)S(1)}, u32[]{:S(2)}, u32[]{:S(2)}) collective-permute-start(bf16[2,48,1536]{2,1,0:T(8,128)(2,1)S(1)} %get-tuple-element.361), channel_id=1, source_target_pairs={{0,2},{1,3},{2,0},{3,1},{4,6},{5,7},{6,4},{7,5},{8,10},{9,11},{10,... | collective-permute-start | bytes 884744 | tf_op jit(solution)/shard_map/ppermute | solution.py:74
  1346.4 69.7 %collective-permute-start.54 = (bf16[2,48,1536]{2,1,0:T(8,128)(2,1)S(1)}, bf16[2,48,1536]{2,1,0:T(8,128)(2,1)S(1)}, u32[]{:S(2)}, u32[]{:S(2)}) collective-permute-start(bf16[2,48,1536]{2,1,0:T(8,128)(2,1)S(1)} %get-tuple-element.362), channel_id=1, source_target_pairs={{0,4},{1,5},{2,6},{3,7},{4,0},{5,1},{6,2},{7,3},{8,12},{9,13},{10,... | collective-permute-start | bytes 884744 | tf_op jit(solution)/shard_map/ppermute | solution.py:74
  1389.0 43.7 %collective-permute-start.76 = (bf16[2,96,768]{2,1,0:T(8,128)(2,1)S(1)}, bf16[2,96,768]{2,1,0:T(8,128)(2,1)S(1)}, u32[]{:S(2)}, u32[]{:S(2)}) collective-permute-start(bf16[2,96,768]{2,1,0:T(8,128)(2,1)S(1)} %get-tuple-element.350), channel_id=1, source_target_pairs={{0,4},{1,5},{2,6},{3,7},{4,0},{5,1},{6,2},{7,3},{8,12},{9,13},{10,... | collective-permute-start | bytes 884744 | tf_op jit(solution)/shard_map/ppermute | solution.py:74
  1416.1 48.5 %collective-permute-start.73 = (bf16[96,768]{1,0:T(8,128)(2,1)S(1)}, bf16[96,768]{1,0:T(8,128)(2,1)S(1)}, u32[]{:S(2)}, u32[]{:S(2)}) collective-permute-start(bf16[96,768]{1,0:T(8,128)(2,1)S(1)} %slice_bitcast_fusion.38), channel_id=1, source_target_pairs={{0,8},{1,9},{2,10},{3,11},{4,12},{5,13},{6,14},{7,15},{8,0},{9,1},... | collective-permute-start | bytes 442376 | tf_op jit(solution)/shard_map/ppermute | solution.py:74
  (132 other events, 1697.0 us)

commit v2 on v1

--- a/solution.py
+++ b/solution.py
@@ -115,6 +115,8 @@
 
 
 def copy_blocks(moves, place, sources, out_shapes):
+    inside, outside = pl.BlockSpec(memory_space=pltpu.VMEM), pl.BlockSpec(memory_space=pl.ANY)
+    from_vmem = len(sources) == 1
     def kernel(place_ref, *refs):
         ins, outs, sems = refs[: len(sources)], refs[len(sources) : -1], refs[-1]
         copies = [
@@ -130,9 +132,10 @@
         kernel,
         out_shape=out_shapes,
         in_specs=[pl.BlockSpec(memory_space=pltpu.SMEM)]
-        + [pl.BlockSpec(memory_space=pl.ANY)] * len(sources),
-        out_specs=[pl.BlockSpec(memory_space=pl.ANY)] * len(out_shapes),
+        + [inside if from_vmem else outside] * len(sources),
+        out_specs=[outside if from_vmem else inside] * len(out_shapes),
         scratch_shapes=[pltpu.SemaphoreType.DMA((lax.axis_size("fsdp"),))],
+        compiler_params=pltpu.CompilerParams(vmem_limit_bytes=24 * 1024 * 1024),
     )(place, *sources)
 
 

time: 1470 us -> 612 us (0.42)
  Pallas kernels: 878 us -> 27.3 us
    pallas_call x6, Pallas kernels: 878 us -> 27.3 us  [copy_blocks(): pl.pallas_call(kernel, out_shape=out_shapes, in_specs=[pl.BlockSpec(memor...]
    unnamed x133 -> x137, local copies, waits for them, and re-layouts: 40.1 us -> 43.9 us
  transfers between devices with their start and end apart: 79 -> 79, of which waited for: 18 -> 19; matrix products, arithmetic and copies ran while one was open for 12% -> 27% of each run, Pallas kernels for 48% -> 3%
where the time goes in v2:
time: 612 us; the launch traced here: 607 us
  local copies, waits for them, and re-layouts  188 us (31%)
  matrix products  170 us (28%)
  waiting for transfers between devices  113 us (18%)
  starting transfers between devices  70.9 us (12%)
  other arithmetic  34.5 us (6%)
  Pallas kernels  27.3 us (4%)
    ppermute x79, waiting for transfers between devices, swap(): return lax.ppermute(array, 'fsdp', flip(mask, lax.axis_size('fsdp')))  113 us
    ppermute x79, starting transfers between devices, swap(): return lax.ppermute(array, 'fsdp', flip(mask, lax.axis_size('fsdp')))  70.9 us
    dot_general x8, matrix products, contract_cols(): lax.dot_general(left, right, (((1,), (1,)), ((), ())), preferred_element_...  47.1 us
    unnamed x137, local copies, waits for them, and re-layouts  43.9 us
    while x36, local copies, waits for them, and re-layouts  37.9 us
    dot_general x7, matrix products, contract_rows(): lax.dot_general(left, right, (((0,), (0,)), ((), ())), preferred_element_...  33.7 us
    dot_general x4, matrix products, masked_scores(): jnp.einsum('qhd,khd->hqk', query_seq, key_seq, preferred_element_type=jnp...  29.7 us
    pallas_call x6, Pallas kernels, copy_blocks(): pl.pallas_call(kernel, out_shape=out_shapes, in_specs=[pl.BlockSpec(memor...  27.3 us
  transfers between devices with their start and end apart: 79, of which 19 were waited for; matrix products, arithmetic and copies ran while one was open for 27% of the time, Pallas kernels for 3%

profile of v2, /device:TPU:0, one launch (start us, length us, event | category | flops | bytes accessed | tf_op | source)
XLA Modules:
  0.0 607.4 jit_solution(3598268194532576318)
XLA Ops:
  27.2 8.5 %collective-permute-done.31 = bf16[96,768]{1,0:T(8,128)(2,1)S(1)} collective-permute-done((bf16[96,768]{1,0:T(8,128)(2,1)}, bf16[96,768]{1,0:T(8,128)(2,1)S(1)}, u32[]{:S(2)}, u32[]{:S(2)}) %collective-permute-start.31) | collective-permute-done | bytes 147488 | tf_op jit(solution)/shard_map/ppermute | solution.py:74
  46.2 7.9 %collective-permute-done.19 = bf16[48,1920]{1,0:T(8,128)(2,1)S(1)} collective-permute-done((bf16[48,1920]{1,0:T(8,128)(2,1)S(1)}, bf16[48,1920]{1,0:T(8,128)(2,1)S(1)}, u32[]{:S(2)}, u32[]{:S(2)}) %collective-permute-start.19) | collective-permute-done | bytes 184352 | tf_op jit(solution)/shard_map/ppermute | solution.py:74
  63.4 8.6 %fusion.57 = f32[262144,12]{0,1:T(8,128)} fusion(bf16[32,12]{0,1:T(8,128)(2,1)S(1)} %copy-done, s32[262144]{0:T(1024)S(1)} %copy-done.38), kind=kOutput, calls=%fused_computation.61 | convolution fusion | flops 209715200 | bytes 13632256 | tf_op jit(solution)/shard_map/dot_general | solution.py:37
  81.6 17.7 %copy.150 = f32[2,8,512,512]{3,2,1,0:T(8,128)} copy(f32[2,8,512,512]{3,1,2,0:T(8,128)} %bitcast.351) | data formatting | bytes 33554432
  99.3 10.7 %slice.376 = f32[12,512,512]{2,1,0:T(8,128)} slice(f32[16,512,512]{2,1,0:T(8,128)} %bitcast.352), slice={[0:12], [0:512], [0:512]} | slice | bytes 25165824 | tf_op jit(solution)/shard_map/reshape | solution.py:383
  110.0 12.6 %copy.108 = f32[12,512,512]{1,2,0:T(8,128)} copy(f32[12,512,512]{2,1,0:T(8,128)} %slice.376) | data formatting | bytes 25165824 | tf_op jit(solution)/shard_map/while | solution.py:413
  178.5 30.0 %while.29 = (s32[]{:T(128)}, bf16[2,512,12,64]{1,3,2,0:T(8,128)(2,1)}, f32[2,12,512]{2,1,0:T(8,128)}, bf16[2,512,12,64]{1,3,2,0:T(8,128)(2,1)}, s32[2]{0:T(128)S...) while((s32[]{:T(128)}, ...), condition=%wide.region_5.6_spmd, body=%wide.region_2.5_spmd.sunk | while | flops 830859776 | bytes 60402892 | solution.py:413
  179.9 8.0 %fusion.182 = (f32[12,512]{1,0:T(8,128)S(1)}, f32[12,512,512]{1,2,0:T(8,128)S(1)}) fusion(f32[12,512,512]{1,2,0:T(8,128)} %get-tuple-element.574, bf16[2,512,12,64]{1,3,2,0:T(8,128)(2,1)} %get-tuple-element.573, s32[]{:T(128)S(6)} %copy.167, bf16[2,512,12,64]{1,3,2,0:T(8,128)(2,1)} %get-tuple-element.572, pred[512]{0:T(512)(128)(4,1)S(1)} %iota_compare_fusion.7), kind=kOutput, calls=%fused_computation.272.clone.1 | convolution fusion | flops 412084224 | bytes 26764800 | tf_op jit(solution)/shard_map/while/body/eval_jaxpr/qhd,khd->hqk/dot_general | solution.py:62
  194.8 8.0 %fusion.182 = (f32[12,512]{1,0:T(8,128)S(1)}, f32[12,512,512]{1,2,0:T(8,128)S(1)}) fusion(f32[12,512,512]{1,2,0:T(8,128)} %get-tuple-element.574, bf16[2,512,12,64]{1,3,2,0:T(8,128)(2,1)} %get-tuple-element.573, s32[]{:T(128)S(6)} %copy.167, bf16[2,512,12,64]{1,3,2,0:T(8,128)(2,1)} %get-tuple-element.572, pred[512]{0:T(512)(128)(4,1)S(1)} %iota_compare_fusion.7), kind=kOutput, calls=%fused_computation.272.clone.1 | convolution fusion | flops 412084224 | bytes 26764800 | tf_op jit(solution)/shard_map/while/body/eval_jaxpr/qhd,khd->hqk/dot_general | solution.py:62
  233.0 11.9 %add_convert_fusion.3 = bf16[1024,768]{0,1:T(8,128)(2,1)} fusion(f32[1024,768]{0,1:T(8,128)} %copy-done.19, bf16[3072,768]{1,0:T(8,128)(2,1)S(1)} %shard_map.214, f32[1024,3072]{1,0:T(8,128)S(1)} %fusion.82), kind=kOutput, calls=%fused_computation.105 | convolution fusion | flops 4861722624 | bytes 22020096 | tf_op jit(solution)/shard_map/dot_general | solution.py:421
  244.9 14.1 %fusion.65 = bf16[1024,3072]{1,0:T(8,128)(2,1)} fusion(f32[1024,3072]{1,0:T(8,128)S(1)} %fusion.82, bf16[3072,768]{1,0:T(8,128)(2,1)S(1)} %shard_map.214, bf16[1024,768]{1,0:T(8,128)(2,1)} %param.28), kind=kOutput, calls=%fused_computation.71 | convolution fusion | flops 4894752768 | bytes 25165824 | tf_op jit(solution)/shard_map/dot_general | solution.py:43
  259.0 9.5 %convolution_convert_fusion.2.refs_0_ = bf16[3072,768]{1,0:T(8,128)(2,1)} fusion(bf16[1024,768]{1,0:T(8,128)(2,1)S(1)} %copy-done.35, f32[1024,3072]{1,0:T(8,128)S(1)} %fusion.82), kind=kOutput, calls=%fused_computation.78 | convolution fusion | flops 4862509056 | bytes 18874368 | tf_op jit(solution)/shard_map/dot_general | solution.py:37
  268.5 9.0 %multiply_reduce_fusion.1 = (f32[768]{0:T(1024)}, f32[1024]{0:T(1024)S(1)}, f32[1024,768]{0,1:T(8,128)S(1)}) fusion(f32[1024,768]{0,1:T(8,128)S(1)} %copy-done.20, f32[1024]{0:T(1024)S(1)} %add_rsqrt_fusion, f32[768]{0:T(1024)S(1)} %copy-done.58, bf16[1024,3072]{1,0:T(8,128)(2,1)} %fusion.65, bf16[768,1536]{1,0:T(8,128)(2,1)S(1)} %copy-done.24, ...), kind=kOutput, calls=%fused_computation.101 | convolution fusion | flops 4845991936 | bytes 17315840 | tf_op jit(solution)/shard_map/dot_general | solution.py:43
  298.5 118.1 %while.30 = (s32[]{:T(128)}, f32[12,32]{1,0:T(8,128)S(1)}, bf16[2,512,12,64]{1,3,2,0:T(8,128)(2,1)}, bf16[2,512,12,64]{1,3,2,0:T(8,128)(2,1)}, bf16[2,512,12,64]...) while((s32[]{:T(128)}, f32[12,32]{1,0:T(8,128)S(1)}, ...), condition=%wide.region_10.11_spmd.clone, body=%wide.region_8.10_spmd.clone.sunk | while | flops 2260856064 | bytes 214574416 | solution.py:463
  323.6 8.7 %copy.157 = bf16[12,512,512]{2,1,0:T(8,128)(2,1)} copy(bf16[12,512,512]{1,2,0:T(8,128)(2,1)} %copy-done.5) | data formatting | bytes 12582912 | tf_op jit(solution)/shard_map/while/body/eval_jaxpr/convert_element_type | solution.py:452
  339.0 11.5 %copy.158 = bf16[2,8,512,512]{3,1,2,0:T(8,128)(2,1)} copy(bf16[2,8,512,512]{3,2,1,0:T(8,128)(2,1)} %bitcast.349) | data formatting | bytes 16777216 | tf_op jit(solution)/shard_map/while
  350.5 7.0 %fusion.195 = f32[12,32]{1,0:T(8,128)S(1)} fusion(bf16[12,262144]{1,0:T(8,128)(2,1)} %bitcast.350, s32[262144]{0:T(1024)S(1)} %copy-done.39, f32[12,32]{1,0:T(8,128)S(1)} %get-tuple-element.593, pred[]{:T(512)S(6)} %compare.5), kind=kOutput, calls=%fused_computation.37.clone.1 | convolution fusion | flops 218104576 | bytes 7343105 | tf_op jit(solution)/shard_map/while/body/eval_jaxpr/dot_general | solution.py:43
  382.4 8.7 %copy.157 = bf16[12,512,512]{2,1,0:T(8,128)(2,1)} copy(bf16[12,512,512]{1,2,0:T(8,128)(2,1)} %copy-done.5) | data formatting | bytes 12582912 | tf_op jit(solution)/shard_map/while/body/eval_jaxpr/convert_element_type | solution.py:452
  397.9 11.5 %copy.158 = bf16[2,8,512,512]{3,1,2,0:T(8,128)(2,1)} copy(bf16[2,8,512,512]{3,2,1,0:T(8,128)(2,1)} %bitcast.349) | data formatting | bytes 16777216 | tf_op jit(solution)/shard_map/while
  409.4 7.0 %fusion.195 = f32[12,32]{1,0:T(8,128)S(1)} fusion(bf16[12,262144]{1,0:T(8,128)(2,1)} %bitcast.350, s32[262144]{0:T(1024)S(1)} %copy-done.39, f32[12,32]{1,0:T(8,128)S(1)} %get-tuple-element.593, pred[]{:T(512)S(6)} %compare.5), kind=kOutput, calls=%fused_computation.37.clone.1 | convolution fusion | flops 218104576 | bytes 7343105 | tf_op jit(solution)/shard_map/while/body/eval_jaxpr/dot_general | solution.py:43
  503.0 10.3 %collective-permute-done.60 = bf16[2,48,1536]{2,1,0:T(8,128)(2,1)S(1)} collective-permute-done((bf16[2,48,1536]{2,1,0:T(8,128)(2,1)S(1)}, bf16[2,48,1536]{2,1,0:T(8,128)(2,1)S(1)}, u32[]{:S(2)}, u32[]{:S(2)}) %collective-permute-start.60) | collective-permute-done | bytes 294944 | tf_op jit(solution)/shard_map/ppermute | solution.py:74
  538.2 10.3 %collective-permute-done.74 = bf16[2,96,768]{2,1,0:T(8,128)(2,1)S(1)} collective-permute-done((bf16[2,96,768]{2,1,0:T(8,128)(2,1)S(1)}, bf16[2,96,768]{2,1,0:T(8,128)(2,1)S(1)}, u32[]{:S(2)}, u32[]{:S(2)}) %collective-permute-start.74) | collective-permute-done | bytes 294944 | tf_op jit(solution)/shard_map/ppermute | solution.py:74
  576.6 13.3 %collective-permute-done.55 = bf16[48,1536]{1,0:T(8,128)(2,1)S(1)} collective-permute-done((bf16[48,1536]{1,0:T(8,128)(2,1)S(1)}, bf16[48,1536]{1,0:T(8,128)(2,1)S(1)}, u32[]{:S(2)}, u32[]{:S(2)}) %collective-permute-start.55) | collective-permute-done | bytes 147488 | tf_op jit(solution)/shard_map/ppermute | solution.py:74
  593.9 9.7 %collective-permute-done.66 = bf16[48,1536]{1,0:T(8,128)(2,1)S(1)} collective-permute-done((bf16[48,1536]{1,0:T(8,128)(2,1)S(1)}, bf16[48,1536]{1,0:T(8,128)(2,1)S(1)}, u32[]{:S(2)}, u32[]{:S(2)}) %collective-permute-start.66) | collective-permute-done | bytes 147488 | tf_op jit(solution)/shard_map/ppermute | solution.py:74
  (481 shorter events, 380.0 us)
Async XLA Ops:
  55.0 72.5 %collective-permute-start.11 = (bf16[4,48,1280]{2,1,0:T(8,128)(2,1)S(1)}, bf16[4,48,1280]{2,1,0:T(8,128)(2,1)}, u32[]{:S(2)}, u32[]{:S(2)}) collective-permute-start(bf16[4,48,1280]{2,1,0:T(8,128)(2,1)S(1)} %pad_maximum_fusion.19.refs_0_), channel_id=1, source_target_pairs={{0,1},{1,0},{2,3},{3,2},{4,5},{5,4},{6,7},{7,6},{8,9},{9,8},{10,11... | collective-permute-start | bytes 1474568 | tf_op jit(solution)/shard_map/ppermute | solution.py:74
  60.8 68.8 %collective-permute-start.13 = (bf16[4,48,1280]{2,1,0:T(8,128)(2,1)}, bf16[4,48,1280]{2,1,0:T(8,128)(2,1)}, u32[]{:S(2)}, u32[]{:S(2)}) collective-permute-start(bf16[4,48,1280]{2,1,0:T(8,128)(2,1)} %collective-permute-done.8.refs_2_), channel_id=1, source_target_pairs={{0,1},{1,0},{2,3},{3,2},{4,5},{5,4},{6,7},{7,6},{8,9},{9,8},{10,11... | collective-permute-start | bytes 1474568 | tf_op jit(solution)/shard_map/ppermute | solution.py:74
  63.4 66.3 %collective-permute-start.12 = (bf16[4,48,1280]{2,1,0:T(8,128)(2,1)}, bf16[4,48,1280]{2,1,0:T(8,128)(2,1)}, u32[]{:S(2)}, u32[]{:S(2)}) collective-permute-start(bf16[4,48,1280]{2,1,0:T(8,128)(2,1)} %collective-permute-done.7.refs_1_), channel_id=1, source_target_pairs={{0,1},{1,0},{2,3},{3,2},{4,5},{5,4},{6,7},{7,6},{8,9},{9,8},{10,11... | collective-permute-start | bytes 1474568 | tf_op jit(solution)/shard_map/ppermute | solution.py:74
  76.6 51.0 %collective-permute-start.14 = (bf16[2,48,1280]{2,1,0:T(8,128)(2,1)S(1)}, bf16[2,48,1280]{2,1,0:T(8,128)(2,1)}, u32[]{:S(2)}, u32[]{:S(2)}) collective-permute-start(bf16[2,48,1280]{2,1,0:T(8,128)(2,1)S(1)} %collective-permute-done.9.refs_3_), channel_id=1, source_target_pairs={{0,1},{1,0},{2,3},{3,2},{4,5},{5,4},{6,7},{7,6},{8,9},{9,8},{10,11... | collective-permute-start | bytes 737288 | tf_op jit(solution)/shard_map/ppermute | solution.py:74
  76.6 52.5 %collective-permute-start.15 = (bf16[2,48,1280]{2,1,0:T(8,128)(2,1)}, bf16[2,48,1280]{2,1,0:T(8,128)(2,1)}, u32[]{:S(2)}, u32[]{:S(2)}) collective-permute-start(bf16[2,48,1280]{2,1,0:T(8,128)(2,1)} %collective-permute-done.10.refs_4_), channel_id=1, source_target_pairs={{0,1},{1,0},{2,3},{3,2},{4,5},{5,4},{6,7},{7,6},{8,9},{9,8},{10,11... | collective-permute-start | bytes 737288 | tf_op jit(solution)/shard_map/ppermute | solution.py:74
  127.5 33.8 %collective-permute-start.37 = (bf16[4,96,768]{2,1,0:T(8,128)(2,1)S(1)}, bf16[4,96,768]{2,1,0:T(8,128)(2,1)}, u32[]{:S(2)}, u32[]{:S(2)}) collective-permute-start(bf16[4,96,768]{2,1,0:T(8,128)(2,1)S(1)} %pad_maximum_fusion.18.refs_0_), channel_id=1, source_target_pairs={{0,1},{1,0},{2,3},{3,2},{4,5},{5,4},{6,7},{7,6},{8,9},{9,8},{10,11... | collective-permute-start | bytes 1769480 | tf_op jit(solution)/shard_map/ppermute | solution.py:74
  127.6 34.2 %collective-permute-start.35 = (bf16[2,96,768]{2,1,0:T(8,128)(2,1)}, bf16[2,96,768]{2,1,0:T(8,128)(2,1)}, u32[]{:S(2)}, u32[]{:S(2)}) collective-permute-start(bf16[2,96,768]{2,1,0:T(8,128)(2,1)} %slice.323), channel_id=1, source_target_pairs={{0,2},{1,3},{2,0},{3,1},{4,6},{5,7},{6,4},{7,5},{8,10},{9,11},{10,... | collective-permute-start | bytes 884744 | tf_op jit(solution)/shard_map/ppermute | solution.py:74
  129.1 34.3 %collective-permute-start.36 = (bf16[2,96,768]{2,1,0:T(8,128)(2,1)}, bf16[2,96,768]{2,1,0:T(8,128)(2,1)}, u32[]{:S(2)}, u32[]{:S(2)}) collective-permute-start(bf16[2,96,768]{2,1,0:T(8,128)(2,1)} %slice.324), channel_id=1, source_target_pairs={{0,4},{1,5},{2,6},{3,7},{4,0},{5,1},{6,2},{7,3},{8,12},{9,13},{10,... | collective-permute-start | bytes 884744 | tf_op jit(solution)/shard_map/ppermute | solution.py:74
  129.6 33.8 %collective-permute-start.39 = (bf16[4,96,768]{2,1,0:T(8,128)(2,1)}, bf16[4,96,768]{2,1,0:T(8,128)(2,1)}, u32[]{:S(2)}, u32[]{:S(2)}) collective-permute-start(bf16[4,96,768]{2,1,0:T(8,128)(2,1)} %collective-permute-done.34.refs_2_), channel_id=1, source_target_pairs={{0,1},{1,0},{2,3},{3,2},{4,5},{5,4},{6,7},{7,6},{8,9},{9,8},{10,11... | collective-permute-start | bytes 1769480 | tf_op jit(solution)/shard_map/ppermute | solution.py:74
  129.6 46.4 %collective-permute-start.38 = (bf16[4,96,768]{2,1,0:T(8,128)(2,1)}, bf16[4,96,768]{2,1,0:T(8,128)(2,1)}, u32[]{:S(2)}, u32[]{:S(2)}) collective-permute-start(bf16[4,96,768]{2,1,0:T(8,128)(2,1)} %collective-permute-done.33.refs_1_), channel_id=1, source_target_pairs={{0,1},{1,0},{2,3},{3,2},{4,5},{5,4},{6,7},{7,6},{8,9},{9,8},{10,11... | collective-permute-start | bytes 1769480 | tf_op jit(solution)/shard_map/ppermute | solution.py:74
  176.1 39.2 %collective-permute-start.25 = (bf16[4,48,1920]{2,1,0:T(8,128)(2,1)S(1)}, bf16[4,48,1920]{2,1,0:T(8,128)(2,1)S(1)}, u32[]{:S(2)}, u32[]{:S(2)}) collective-permute-start(bf16[4,48,1920]{2,1,0:T(8,128)(2,1)S(1)} %pad_maximum_fusion.17.refs_0_), channel_id=1, source_target_pairs={{0,1},{1,0},{2,3},{3,2},{4,5},{5,4},{6,7},{7,6},{8,9},{9,8},{10,11... | collective-permute-start | bytes 2211848 | tf_op jit(solution)/shard_map/ppermute | solution.py:74
  176.1 39.2 %collective-permute-start.27 = (bf16[4,48,1920]{2,1,0:T(8,128)(2,1)S(1)}, bf16[4,48,1920]{2,1,0:T(8,128)(2,1)}, u32[]{:S(2)}, u32[]{:S(2)}) collective-permute-start(bf16[4,48,1920]{2,1,0:T(8,128)(2,1)S(1)} %collective-permute-done.22.refs_2_), channel_id=1, source_target_pairs={{0,1},{1,0},{2,3},{3,2},{4,5},{5,4},{6,7},{7,6},{8,9},{9,8},{10,11... | collective-permute-start | bytes 2211848 | tf_op jit(solution)/shard_map/ppermute | solution.py:74
  176.6 38.7 %collective-permute-start.26 = (bf16[4,48,1920]{2,1,0:T(8,128)(2,1)S(1)}, bf16[4,48,1920]{2,1,0:T(8,128)(2,1)}, u32[]{:S(2)}, u32[]{:S(2)}) collective-permute-start(bf16[4,48,1920]{2,1,0:T(8,128)(2,1)S(1)} %collective-permute-done.21.refs_1_), channel_id=1, source_target_pairs={{0,1},{1,0},{2,3},{3,2},{4,5},{5,4},{6,7},{7,6},{8,9},{9,8},{10,11... | collective-permute-start | bytes 2211848 | tf_op jit(solution)/shard_map/ppermute | solution.py:74
  176.7 38.6 %collective-permute-start.28 = (bf16[2,48,1920]{2,1,0:T(8,128)(2,1)}, bf16[2,48,1920]{2,1,0:T(8,128)(2,1)}, u32[]{:S(2)}, u32[]{:S(2)}) collective-permute-start(bf16[2,48,1920]{2,1,0:T(8,128)(2,1)} %collective-permute-done.23.refs_3_), channel_id=1, source_target_pairs={{0,1},{1,0},{2,3},{3,2},{4,5},{5,4},{6,7},{7,6},{8,9},{9,8},{10,11... | collective-permute-start | bytes 1105928 | tf_op jit(solution)/shard_map/ppermute | solution.py:74
  177.1 38.2 %collective-permute-start.29 = (bf16[2,48,1920]{2,1,0:T(8,128)(2,1)}, bf16[2,48,1920]{2,1,0:T(8,128)(2,1)}, u32[]{:S(2)}, u32[]{:S(2)}) collective-permute-start(bf16[2,48,1920]{2,1,0:T(8,128)(2,1)} %collective-permute-done.24.refs_4_), channel_id=1, source_target_pairs={{0,1},{1,0},{2,3},{3,2},{4,5},{5,4},{6,7},{7,6},{8,9},{9,8},{10,11... | collective-permute-start | bytes 1105928 | tf_op jit(solution)/shard_map/ppermute | solution.py:74
  453.1 28.9 %collective-permute-start.47 = (bf16[4,4,48,1536]{3,2,1,0:T(8,128)(2,1)}, bf16[4,4,48,1536]{3,2,1,0:T(8,128)(2,1)}, u32[]{:S(2)}, u32[]{:S(2)}) collective-permute-start(bf16[4,4,48,1536]{3,2,1,0:T(8,128)(2,1)} %get-tuple-element.137), channel_id=1, source_target_pairs={{0,1},{1,0},{2,3},{3,2},{4,5},{5,4},{6,7},{7,6},{8,9},{9,8},{10,11... | collective-permute-start | bytes 7077896 | tf_op jit(solution)/shard_map/ppermute | solution.py:74
  460.6 28.1 %collective-permute-start.69 = (bf16[4,4,96,768]{3,2,1,0:T(8,128)(2,1)}, bf16[4,4,96,768]{3,2,1,0:T(8,128)(2,1)}, u32[]{:S(2)}, u32[]{:S(2)}) collective-permute-start(bf16[4,4,96,768]{3,2,1,0:T(8,128)(2,1)} %get-tuple-element.141), channel_id=1, source_target_pairs={{0,1},{1,0},{2,3},{3,2},{4,5},{5,4},{6,7},{7,6},{8,9},{9,8},{10,11... | collective-permute-start | bytes 7077896 | tf_op jit(solution)/shard_map/ppermute | solution.py:74
  485.2 31.3 %collective-permute-start.48 = (bf16[2,48,1536]{2,1,0:T(8,128)(2,1)S(1)}, bf16[2,48,1536]{2,1,0:T(8,128)(2,1)S(1)}, u32[]{:S(2)}, u32[]{:S(2)}) collective-permute-start(bf16[2,48,1536]{2,1,0:T(8,128)(2,1)S(1)} %get-tuple-element.361), channel_id=1, source_target_pairs={{0,2},{1,3},{2,0},{3,1},{4,6},{5,7},{6,4},{7,5},{8,10},{9,11},{10,... | collective-permute-start | bytes 884744 | tf_op jit(solution)/shard_map/ppermute | solution.py:74
  486.7 69.8 %collective-permute-start.54 = (bf16[2,48,1536]{2,1,0:T(8,128)(2,1)S(1)}, bf16[2,48,1536]{2,1,0:T(8,128)(2,1)S(1)}, u32[]{:S(2)}, u32[]{:S(2)}) collective-permute-start(bf16[2,48,1536]{2,1,0:T(8,128)(2,1)S(1)} %get-tuple-element.362), channel_id=1, source_target_pairs={{0,4},{1,5},{2,6},{3,7},{4,0},{5,1},{6,2},{7,3},{8,12},{9,13},{10,... | collective-permute-start | bytes 884744 | tf_op jit(solution)/shard_map/ppermute | solution.py:74
  488.2 28.6 %collective-permute-start.52 = (bf16[2,48,1536]{2,1,0:T(8,128)(2,1)S(1)}, bf16[2,48,1536]{2,1,0:T(8,128)(2,1)S(1)}, u32[]{:S(2)}, u32[]{:S(2)}) collective-permute-start(bf16[2,48,1536]{2,1,0:T(8,128)(2,1)S(1)} %get-tuple-element.363), channel_id=1, source_target_pairs={{0,4},{1,5},{2,6},{3,7},{4,0},{5,1},{6,2},{7,3},{8,12},{9,13},{10,... | collective-permute-start | bytes 884744 | tf_op jit(solution)/shard_map/ppermute | solution.py:74
  528.9 42.9 %collective-permute-start.76 = (bf16[2,96,768]{2,1,0:T(8,128)(2,1)S(1)}, bf16[2,96,768]{2,1,0:T(8,128)(2,1)S(1)}, u32[]{:S(2)}, u32[]{:S(2)}) collective-permute-start(bf16[2,96,768]{2,1,0:T(8,128)(2,1)S(1)} %get-tuple-element.350), channel_id=1, source_target_pairs={{0,4},{1,5},{2,6},{3,7},{4,0},{5,1},{6,2},{7,3},{8,12},{9,13},{10,... | collective-permute-start | bytes 884744 | tf_op jit(solution)/shard_map/ppermute | solution.py:74
  548.5 27.7 %collective-permute-start.51 = (bf16[48,1536]{1,0:T(8,128)(2,1)S(1)}, bf16[48,1536]{1,0:T(8,128)(2,1)S(1)}, u32[]{:S(2)}, u32[]{:S(2)}) collective-permute-start(bf16[48,1536]{1,0:T(8,128)(2,1)S(1)} %slice_bitcast_fusion.46), channel_id=1, source_target_pairs={{0,8},{1,9},{2,10},{3,11},{4,12},{5,13},{6,14},{7,15},{8,0},{9,1},... | collective-permute-start | bytes 442376 | tf_op jit(solution)/shard_map/ppermute | solution.py:74
  556.5 47.8 %collective-permute-start.73 = (bf16[96,768]{1,0:T(8,128)(2,1)S(1)}, bf16[96,768]{1,0:T(8,128)(2,1)S(1)}, u32[]{:S(2)}, u32[]{:S(2)}) collective-permute-start(bf16[96,768]{1,0:T(8,128)(2,1)S(1)} %slice_bitcast_fusion.38), channel_id=1, source_target_pairs={{0,8},{1,9},{2,10},{3,11},{4,12},{5,13},{6,14},{7,15},{8,0},{9,1},... | collective-permute-start | bytes 442376 | tf_op jit(solution)/shard_map/ppermute | solution.py:74
  576.2 28.1 %collective-permute-start.77 = (bf16[96,768]{1,0:T(8,128)(2,1)S(1)}, bf16[96,768]{1,0:T(8,128)(2,1)S(1)}, u32[]{:S(2)}, u32[]{:S(2)}) collective-permute-start(bf16[96,768]{1,0:T(8,128)(2,1)S(1)} %get-tuple-element.373), channel_id=1, source_target_pairs={{0,16},{1,17},{2,18},{3,19},{4,20},{5,21},{6,22},{7,23},{8,24},{9,... | collective-permute-start | bytes 442376 | tf_op jit(solution)/shard_map/ppermute | solution.py:74
  (134 other events, 1271.6 us)

commit v3 on v0

v3 whole, which is shorter than its diff:
```python
import functools
import math

import jax
import jax.numpy as jnp
import numpy as np
from jax import lax
from jax.experimental import pallas as pl
from jax.experimental.pallas import tpu as pltpu
from jax.sharding import PartitionSpec as P

NB = 32
MAXD = 128
SEQ = 512
MIB = 1024 * 1024


def bucket_ids(span_length):
    offset = np.arange(span_length)[None, :] - np.arange(span_length)[:, None]
    half_count = NB // 2
    exact_count = half_count // 2
    result = np.where(offset > 0, half_count, 0)
    distance = np.abs(offset)
    spread = exact_count + np.floor(
        np.log(np.maximum(distance, 1) / exact_count)
        / math.log(MAXD / exact_count)
        * (half_count - exact_count)
    )
    spread = np.minimum(spread, half_count - 1)
    result = result + np.where(distance < exact_count, distance, spread)
    return result.astype(np.int32)


def flip(mask, count):
    return [(i, i ^ mask) for i in range(count)]


def swap(array, mask):
    return lax.ppermute(array, "fsdp", flip(mask, lax.axis_size("fsdp")))


def gather_chips(unit):
    line = lax.axis_size("fsdp") // 8
    half = line // 2
    near = jnp.stack([unit] + [swap(unit, 8 * hop) for hop in range(1, line)])
    over_x, over_y = swap(near, 2), swap(near, 4)
    return (near, over_x, over_y, swap(over_y[:half], 2), swap(over_x[half:], 4))


def chip_distances():
    line = lax.axis_size("fsdp") // 8
    half = line // 2
    blocks = []
    for part, (plane, first, last) in enumerate(
        ((0, 0, line), (1, 0, line), (2, 0, line), (3, 0, half), (3, half, line))
    ):
        blocks += [(part, hop - first, 4 * hop + plane) for hop in range(first, last)]
    return blocks


def scatter_chips(send, keep):
    line = keep.shape[1]
    half = line // 2

    def add(*terms):
        return sum(term.astype(jnp.float32) for term in terms)

    def low(value):
        return value.astype(jnp.bfloat16)

    both = low(add(keep, swap(send, 1)))
    via_x, via_y = swap(both[3, :half], 2), swap(both[3, half:], 4)
    x_low, y_high = swap(both[1, :half], 2), swap(both[2, half:], 4)
    y_low = swap(low(add(both[2, :half], via_x)), 4)
    x_high = swap(low(add(both[1, half:], via_y)), 2)
    total = jnp.concatenate(
        [low(add(both[0, :half], x_low, y_low)), low(add(both[0, half:], x_high, y_high))]
    )
    return add(total[0], *[swap(total[hop], 8 * hop) for hop in range(1, line)])


def both_cores(parts):
    return parts + tuple(swap(part, 1) for part in parts)


def chip_unit(shard, core):
    half = shard.shape[1] // 2
    mine = lax.dynamic_slice_in_dim(shard, core * half, half, 1)
    other = swap(lax.dynamic_slice_in_dim(shard, (1 - core) * half, half, 1), 1)
    return jnp.where(
        core == 0, jnp.concatenate([mine, other], 0), jnp.concatenate([other, mine], 0)
    )


def own_rows(chip_sum, core):
    rows = chip_sum.shape[0] // 2
    mine = lax.dynamic_slice_in_dim(chip_sum, core * rows, rows, 0)
    other = swap(lax.dynamic_slice_in_dim(chip_sum, (1 - core) * rows, rows, 0), 1)
    return mine, other


def join_columns(mine, other, core):
    return jnp.where(
        core == 0, jnp.concatenate([mine, other], 1), jnp.concatenate([other, mine], 1)
    )


def halves_of(*arrays):
    return jnp.stack(
        [
            jnp.concatenate(
                [
                    array[:, part * array.shape[1] // 2 : (part + 1) * array.shape[1] // 2]
                    for array in arrays
                ],
                1,
            )
            for part in range(2)
        ]
    )


def sum_plain(half_attn, half_in, grad_out):
    side = half_attn.shape[-1] // 4

    def owned(array):
        return lax.psum_scatter(
            array.astype(jnp.float32), "fsdp", scatter_dimension=0, tiled=True
        )

    grads = [
        jnp.concatenate([part[0], part[1]], 1)
        for part in [half_attn[:, :, k * side : (k + 1) * side] for k in range(4)] + [half_in]
    ]
    return [owned(grad) for grad in grads + [grad_out]]


def sum_everywhere(vector):
    mask = 1
    while mask < lax.axis_size("fsdp"):
        vector = vector + swap(vector, mask)
        mask *= 2
    return vector


def nn(left, right):
    return lax.dot_general(
        left, right, (((1,), (0,)), ((), ())), preferred_element_type=jnp.float32
    )


def nt(left, right):
    return lax.dot_general(
        left, right, (((1,), (1,)), ((), ())), preferred_element_type=jnp.float32
    )


def tn(left, right):
    return lax.dot_general(
        left, right, (((0,), (0,)), ((), ())), preferred_element_type=jnp.float32
    )


def low(value):
    return value.astype(jnp.bfloat16)


def wide(value):
    return value.astype(jnp.float32)


def norm_scale(values):
    return lax.rsqrt(jnp.mean(values * values, axis=-1, keepdims=True) + 1e-06)


def rms_back(scaled, scale, gain, grad_normed):
    weighted = grad_normed * gain
    return scale * (weighted - scaled * jnp.mean(weighted * scaled, axis=-1, keepdims=True))


IN_HBM = pl.BlockSpec(memory_space=pl.ANY)
IN_SMEM = pl.BlockSpec(memory_space=pltpu.SMEM)
IN_VMEM = pl.BlockSpec(memory_space=pltpu.VMEM)


def cost(flops, bytes_moved):
    return pl.CostEstimate(flops=flops, bytes_accessed=bytes_moved, transcendentals=0)


def plan(me, rows, by_chips, side, per_core):
    chip, core = me // 2, me % 2
    if not by_chips:
        return []
    count = 5
    found = []
    for part, index, distance in chip_distances():
        number = chip ^ distance
        if per_core:
            number = number * 2 + (core ^ side)
        found.append((side * count + part, index, pl.multiple_of(number * rows, 16)))
    return found


def column_copies(me, sources, target, sems, side, by_chips, columns):
    first, last = columns
    if not by_chips:
        half = (me % 2) ^ side
        return [
            pltpu.make_async_copy(sources[0].at[half, :, pl.ds(first, last - first)], target, sems.at[0])
        ]
    rows = sources[0].shape[1]
    return [
        pltpu.make_async_copy(
            sources[part].at[index, :, pl.ds(first, last - first)],
            target.at[pl.ds(start, rows), :],
            sems.at[number],
        )
        for number, (part, index, start) in enumerate(plan(me, rows, True, side, False))
    ]


def row_copies(me, sources, target, sems, side, by_chips):
    if not by_chips:
        half = target.shape[0] // 2
        where = pl.ds(side * half, half)
        return [pltpu.make_async_copy(sources[0].at[where, :], target.at[where, :], sems.at[0])]
    rows = sources[0].shape[1]
    return [
        pltpu.make_async_copy(
            sources[part].at[index], target.at[pl.ds(start, rows), :], sems.at[number]
        )
        for number, (part, index, start) in enumerate(plan(me, rows, True, side, True))
    ]


def start_all(copies):
    for copy in copies:
        copy.start()


def wait_all(copies):
    for copy in copies:
        copy.wait()


def half_copies(me, tile, targets, sems, side, by_chips, columns):
    first, count = columns
    if not by_chips:
        half = (me % 2) ^ side
        return [
            pltpu.make_async_copy(tile, targets[0].at[half, :, pl.ds(first, count)], sems.at[0])
        ]
    planes, line, rows = targets[side].shape[:3]
    chip = me // 2
    return [
        pltpu.make_async_copy(
            tile.at[pl.ds(pl.multiple_of((chip ^ (4 * hop + plane)) * rows, 16), rows), :],
            targets[side].at[plane, hop, :, pl.ds(first, count)],
            sems.at[plane * line + hop],
        )
        for plane in range(planes)
        for hop in range(line)
    ]


def strip_copies(me, tile, targets, sems, strip, by_chips):
    if not by_chips:
        rows = tile.shape[0]
        return [
            pltpu.make_async_copy(
                tile, targets[0].at[pl.ds(pl.multiple_of(strip * rows, 16), rows), :], sems.at[0]
            )
        ]
    planes, line, rows = targets[0].shape[:3]
    chip, core = me // 2, me % 2
    return [
        pltpu.make_async_copy(
            tile.at[
                pl.ds(pl.multiple_of((((chip % 4) ^ plane) * 2 + (core ^ side)) * rows, 16), rows), :
            ],
            targets[side].at[plane, (chip // 4) ^ strip],
            sems.at[side * planes + plane],
        )
        for side in range(2)
        for plane in range(planes)
    ]


def bias_planes(table):
    heads = table.shape[1]
    ids = bucket_ids(SEQ)
    flat = np.concatenate([ids[:, 0], ids[0, :1], ids[0, :0:-1]])
    onehot = (np.arange(table.shape[0])[:, None] == flat[None, :]).astype(np.float32)
    rows = lax.dot_general(
        wide(table), jnp.asarray(onehot), (((0,), (0,)), ((), ())), precision=lax.Precision.HIGHEST
    )

    def kernel(rows_ref, plane_ref):
        row = rows_ref[pl.ds(pl.program_id(0), 1), :]
        spread = jnp.broadcast_to(row, (SEQ, 2 * SEQ))
        moved = pltpu.roll(spread, 0, 1, stride=1, stride_axis=0)
        plane_ref[0] = low(moved[:, :SEQ])

    return pl.pallas_call(
        kernel,
        grid=(heads,),
        out_shape=jax.ShapeDtypeStruct((heads, SEQ, SEQ), jnp.bfloat16),
        in_specs=[IN_VMEM],
        out_specs=pl.BlockSpec((1, SEQ, SEQ), lambda head: (head, 0, 0)),
        compiler_params=pltpu.CompilerParams(vmem_limit_bytes=24 * MIB),
    )(rows)


def line_ids():
    ids = bucket_ids(SEQ)
    ahead = (np.arange(2 * SEQ)[None, :] - np.arange(8)[:, None] - (SEQ - 128) + SEQ) % (2 * SEQ)
    ahead = ahead - SEQ
    return np.where(ahead >= 0, ids[np.maximum(ahead, 0), 0], ids[0, np.minimum(-ahead, SEQ - 1)])


def project_qkv(place, tokens, sources, by_chips):
    slots, width = tokens.shape
    side_cols = width // 2
    packed = sources[0].shape[-1]
    block = 256
    steps = slots // block

    def kernel(place_ref, x_ref, *refs):
        ins = refs[: len(sources)]
        q_ref, k_ref, v_ref, gains_ref, weights, normed, sems = refs[len(sources) :]
        side, step = pl.program_id(0), pl.program_id(1)
        me = place_ref[0]

        def copies(which):
            return column_copies(
                me, ins, weights.at[which], sems.at[which], which, by_chips, (0, packed)
            )

        @pl.when((side == 0) & (step == 0))
        def _():
            start_all(copies(0))
            start_all(copies(1))
            wait_all(copies(0))
            gains = jnp.transpose(wide(weights[0, :, 3 * side_cols :]))
            gains_ref[...] = gains[:8]

            def normalise(index, carry):
                where = pl.ds(pl.multiple_of(index * 128, 128), 128)
                rows = wide(x_ref[where, :])
                normed[where, :] = low(rows * norm_scale(rows) * gains[:1])
                return carry

            lax.fori_loop(0, slots // 128, normalise, 0)

        @pl.when((side == 1) & (step == 0))
        def _():
            wait_all(copies(1))

        rows = normed[pl.ds(pl.multiple_of(step * block, block), block), :]
        for part, out in enumerate((q_ref, k_ref, v_ref)):
            out[...] = low(nn(rows, weights[side, :, part * side_cols : (part + 1) * side_cols]))

    flat = jax.ShapeDtypeStruct((slots, width), jnp.bfloat16)
    out_block = pl.BlockSpec(
        (block, side_cols), lambda side, step, place_ref: (step, (place_ref[0] % 2) ^ side)
    )
    return pl.pallas_call(
        kernel,
        grid_spec=pltpu.PrefetchScalarGridSpec(
            num_scalar_prefetch=1,
            grid=(2, steps),
            in_specs=[pl.BlockSpec((slots, width), lambda side, step, place_ref: (0, 0))]
            + [IN_HBM] * len(sources),
            out_specs=[out_block] * 3
            + [pl.BlockSpec((8, width), lambda side, step, place_ref: (0, 0))],
            scratch_shapes=[
                pltpu.VMEM((2, width, packed), jnp.bfloat16),
                pltpu.VMEM((slots, width), jnp.bfloat16),
                pltpu.SemaphoreType.DMA((2, 16)),
            ],
        ),
        out_shape=[flat] * 3 + [jax.ShapeDtypeStruct((8, width), jnp.float32)],
        compiler_params=pltpu.CompilerParams(vmem_limit_bytes=40 * MIB),
        cost_estimate=cost(6 * slots * width * width, 12 * slots * width),
    )(place, tokens, *sources)


def attend(valid, query, key, value, planes, first, count):
    slots, width = query.shape
    seqs = slots // SEQ
    heads = planes.shape[0]
    pair_cols = 2 * width // heads
    head_size = pair_cols // 2
    piece = 256

    def kernel(valid_ref, q_ref, k_ref, v_ref, planes_ref, out_ref, prob_ref):
        seq = pl.program_id(1)
        limit = valid_ref[seq]
        permitted = lax.broadcasted_iota(jnp.int32, (SEQ, 1), 0) < limit
        own_lane = lax.broadcasted_iota(jnp.int32, (1, pair_cols), 1) < head_size
        keys, values = k_ref[...], v_ref[...]
        zero = jnp.zeros((), jnp.bfloat16)
        value_cols = low(jnp.transpose(wide(values)))
        for part in range(SEQ // piece):
            where = slice(part * piece, (part + 1) * piece)
            mixed = []
            for head in range(2):
                mask = own_lane if head == 0 else ~own_lane
                scores = nt(jnp.where(mask, keys, zero), q_ref[where, :])
                scores = scores + wide(planes_ref[head, :, where])
                scores = jnp.where(permitted, scores, -1e30)
                peak = jnp.max(scores, axis=0, keepdims=True)
                raised = jnp.exp(scores - peak)
                total = jnp.sum(raised, axis=0, keepdims=True)
                prob = low(raised * (1.0 / total))
                prob_ref[0, head, :, where] = prob
                mixed.append(nn(value_cols[head * head_size : (head + 1) * head_size], prob))
            out_ref[where, :] = low(jnp.transpose(jnp.concatenate(mixed, 0)))

    def cols(pair, seq, valid_ref):
        return (seq, first + pair)

    block = pl.BlockSpec((SEQ, pair_cols), cols)
    return pl.pallas_call(
        kernel,
        grid_spec=pltpu.PrefetchScalarGridSpec(
            num_scalar_prefetch=1,
            grid=(count, seqs),
            in_specs=[
                block,
                block,
                block,
                pl.BlockSpec((2, SEQ, SEQ), lambda pair, seq, valid_ref: (first + pair, 0, 0)),
            ],
            out_specs=[
                pl.BlockSpec((SEQ, pair_cols), lambda pair, seq, valid_ref: (seq, pair)),
                pl.BlockSpec(
                    (1, 2, SEQ, SEQ), lambda pair, seq, valid_ref: (seq, pair, 0, 0)
                ),
            ],
        ),
        out_shape=[
            jax.ShapeDtypeStruct((slots, count * pair_cols), jnp.bfloat16),
            jax.ShapeDtypeStruct((seqs, 2 * count, SEQ, SEQ), jnp.bfloat16),
        ],
        compiler_params=pltpu.CompilerParams(vmem_limit_bytes=40 * MIB),
        cost_estimate=cost(count * slots * SEQ * 2048, count * slots * SEQ * 8),
    )(valid, query, key, value, planes)


def attend_back(query, key, value, grad_mixed, prob, first, count, heads):
    slots, width = query.shape
    seqs = slots // SEQ
    pair_cols = 2 * width // heads
    head_size = pair_cols // 2
    piece = 256

    def kernel(q_ref, k_ref, v_ref, g_ref, prob_ref, dq_ref, dk_ref, dv_ref, table_ref, planes):
        seq = pl.program_id(1)
        own_lane = lax.broadcasted_iota(jnp.int32, (1, pair_cols), 1) < head_size
        values = v_ref[...]
        zero = jnp.zeros((), jnp.bfloat16)
        key_cols = low(jnp.transpose(wide(k_ref[...])))
        dk, dv, dq = [], [], [[], []]
        for head in range(2):
            mask = own_lane if head == 0 else ~own_lane
            masked = jnp.where(mask, values, zero)
            sum_k = sum_v = 0.0
            for part in range(SEQ // piece):
                where = slice(part * piece, (part + 1) * piece)
                prob = prob_ref[0, head, :, where]
                grads = g_ref[where, :]
                sum_v += nn(prob, grads)
                prob = wide(prob)
                grad_prob = nt(masked, grads)
                weighted = prob * grad_prob
                dot = jnp.sum(weighted, axis=0, keepdims=True)
                grad_scores = weighted - prob * dot

                @pl.when(seq == 0)
                def _():
                    planes[head, :, where] = grad_scores

                @pl.when(seq > 0)
                def _():
                    planes[head, :, where] += grad_scores

                grad_scores = low(grad_scores)
                sum_k += nn(grad_scores, q_ref[where, :])
                dq[part].append(
                    nn(key_cols[head * head_size : (head + 1) * head_size], grad_scores)
                )
            dk.append(sum_k)
            dv.append(sum_v)
        dk_ref[...] = low(jnp.where(own_lane, dk[0], dk[1]))
        dv_ref[...] = low(jnp.where(own_lane, dv[0], dv[1]))
        for part in range(SEQ // piece):
            dq_ref[part * piece : (part + 1) * piece, :] = low(
                jnp.transpose(jnp.concatenate(dq[part], 0))
            )

        @pl.when(seq == seqs - 1)
        def _():
            for head in range(2):
                lined = jnp.zeros((8, 2 * SEQ), jnp.float32)
                for low_row in range(0, 128, 8):
                    frame = jnp.zeros((8, 2 * SEQ), jnp.float32)
                    for high_row in range(0, SEQ, 128):
                        rows = planes[head, high_row + low_row : high_row + low_row + 8, :]
                        ahead = SEQ - 128 - high_row
                        filled = [rows, jnp.zeros((8, SEQ - ahead), jnp.float32)]
                        if ahead:
                            filled = [jnp.zeros((8, ahead), jnp.float32)] + filled
                        frame = frame + jnp.concatenate(filled, 1)
                    if low_row:
                        frame = pltpu.roll(frame, 2 * SEQ - low_row, 1)
                    lined = lined + frame
                table_ref[0, head] = lined

    def cols(pair, seq):
        return (seq, first + pair)

    def own_cols(pair, seq):
        return (seq, pair)

    block = pl.BlockSpec((SEQ, pair_cols), cols)
    own_block = pl.BlockSpec((SEQ, pair_cols), own_cols)
    flat = jax.ShapeDtypeStruct((slots, count * pair_cols), jnp.bfloat16)
    return pl.pallas_call(
        kernel,
        grid=(count, seqs),
        in_specs=[
            block,
            block,
            block,
            block,
            pl.BlockSpec((1, 2, SEQ, SEQ), lambda pair, seq: (seq, pair, 0, 0)),
        ],
        out_specs=[own_block] * 3
        + [pl.BlockSpec((1, 2, 8, 2 * SEQ), lambda pair, seq: (pair, 0, 0, 0))],
        out_shape=[flat] * 3 + [jax.ShapeDtypeStruct((count, 2, 8, 2 * SEQ), jnp.float32)],
        scratch_shapes=[pltpu.VMEM((2, SEQ, SEQ), jnp.float32)],
        compiler_params=pltpu.CompilerParams(vmem_limit_bytes=40 * MIB),
        cost_estimate=cost(count * slots * SEQ * 4096, count * slots * SEQ * 8),
    )(query, key, value, grad_mixed, prob)


def feed_forward(place, tokens, attended, cotangent, gains, in_sources, out_sources, by_chips):
    slots, width = tokens.shape
    side_cols = width // 2
    hidden_cols = 2 * (in_sources[0].shape[-1] - side_cols)
    block = 256
    blocks = slots // block
    chunk = 768
    per_side = hidden_cols // 2 // chunk
    count_att = len(attended)
    root, bend = math.sqrt(2.0 / math.pi), 0.044715

    def kernel(place_ref, x_hbm, cot_hbm, gains_ref, *refs):
        refs = list(refs)

        def take(number):
            taken, refs[:] = refs[:number], refs[number:]
            return taken

        att_hbm, in_hbm, out_hbm = take(count_att), take(len(in_sources)), take(len(out_sources))
        y_hbm, grad_hbm, back_hbm = take(3)
        in_targets = take(2 if by_chips else 1)
        out_targets = take(2 if by_chips else 1)
        (gain_out,) = take(1)
        x, att, cot, w_o, w_in, w_out, hidden, normed, flipped = take(9)
        sum_y, sum_g, act, grad_pre, tile_in, tile_out = take(6)
        load_sems, o_sems, in_sems, out_sems, store_sems, tile_in_sems, tile_out_sems = take(7)
        me = place_ref[0]
        core = me % 2
        gain = gains_ref[1:2, :]

        def rows_of(index):
            return pl.ds(pl.multiple_of(index * block, block), block)

        loads = [
            pltpu.make_async_copy(x_hbm, x, load_sems.at[0]),
            pltpu.make_async_copy(cot_hbm, cot, load_sems.at[1]),
        ]
        cols = 0
        for number, source in enumerate(att_hbm):
            loads.append(
                pltpu.make_async_copy(
                    source, att.at[:, pl.ds(cols, source.shape[1])], load_sems.at[2 + number]
                )
            )
            cols += source.shape[1]
        o_loads, in_loads, out_loads = [], [], []
        for side in range(2):
            o_cols = pl.ds(pl.multiple_of((core ^ side) * side_cols, 128), side_cols)
            o_loads += column_copies(
                me, in_hbm, w_o.at[:, o_cols], o_sems.at[side], side, by_chips, (0, side_cols)
            )
            in_loads.append(
                column_copies(
                    me,
                    in_hbm,
                    w_in.at[side],
                    in_sems.at[side],
                    side,
                    by_chips,
                    (side_cols, in_sources[0].shape[-1]),
                )
            )
            out_loads += row_copies(me, out_hbm, w_out, out_sems.at[side], side, by_chips)
        start_all(loads)
        start_all(o_loads)
        start_all(in_loads[0])
        start_all(out_loads)
        start_all(in_loads[1])
        wait_all(loads)
        wait_all(o_loads)

        def before(index, carry):
            where = rows_of(index)
            value = wide(x[where, :]) + nn(att[where, :], w_o[...])
            hidden[where, :] = value
            rows = value * norm_scale(value) * gain
            normed[where, :] = low(rows)
            flipped[:, where] = low(jnp.transpose(rows))
            sum_y[where, :] = value
            sum_g[where, :] = jnp.zeros_like(value)
            return carry

        lax.fori_loop(0, blocks, before, 0)
        wait_all(in_loads[0])
        wait_all(out_loads)

        stores = []
        for side in range(2):
            if side:
                wait_all(in_loads[1])
            for part in range(per_side):
                number = side * per_side + part
                strip = (core ^ side) * per_side + part
                unit_rows = pl.ds(pl.multiple_of(strip * chunk, chunk), chunk)
                unit_cols = slice(part * chunk, (part + 1) * chunk)

                def through(index, carry):
                    where = rows_of(index)
                    pre = nn(normed[where, :], w_in[side, :, unit_cols])
                    square = pre * pre
                    slope = jnp.tanh(root * pre * (1.0 + bend * square))
                    opened = 0.5 * (1.0 + slope)
                    gate = opened + (0.5 * root) * pre * (1.0 - slope * slope) * (
                        1.0 + (3.0 * bend) * square
                    )
                    acted = low(pre * opened)
                    act[where, :] = acted
                    back = low(nt(cot[where, :], w_out[unit_rows, :]) * gate)
                    grad_pre[where, :] = back
                    sum_y[where, :] += nn(acted, w_out[unit_rows, :])
                    sum_g[where, :] += nt(back, w_in[side, :, unit_cols])
                    return carry

                lax.fori_loop(0, blocks, through, 0)
                slot = number % 2
                if number >= 2:
                    wait_all(stores[number - 2])
                for third in range(3):
                    some = slice(third * chunk // 3, (third + 1) * chunk // 3)
                    tile_out[slot, some, :] = low(tn(act[:, some], cot[...]))
                for third in range(3):
                    some = slice(third * width // 3, (third + 1) * width // 3)
                    tile_in[slot, some, :] = low(nn(flipped[some, :], grad_pre[...]))
                copies = strip_copies(
                    me, tile_out.at[slot], out_targets, tile_out_sems.at[slot], strip, by_chips
                ) + half_copies(
                    me,
                    tile_in.at[slot],
                    in_targets,
                    tile_in_sems.at[slot],
                    side,
                    by_chips,
                    (side_cols + part * chunk, chunk),
                )
                start_all(copies)
                stores.append(copies)

        def after(index, carry):
            where = rows_of(index)
            value = hidden[where, :]
            normed[where, :] = low(sum_y[where, :])
            scale = norm_scale(value)
            scaled = value * scale
            grad = sum_g[where, :]
            gains_sum = carry + jnp.sum(grad * scaled, axis=0, keepdims=True)
            grad = wide(cot[where, :]) + rms_back(scaled, scale, gain, grad)
            sum_g[where, :] = grad
            branch = low(grad)
            grad_pre[where, :] = branch
            act[where, :] = low(nt(branch, w_o[...]))
            return gains_sum

        gain_sum = lax.fori_loop(0, blocks, after, jnp.zeros((1, width), jnp.float32))
        gain_out[...] = jnp.broadcast_to(gain_sum, gain_out.shape)
        last = [
            pltpu.make_async_copy(normed, y_hbm, store_sems.at[0]),
            pltpu.make_async_copy(sum_g, grad_hbm, store_sems.at[1]),
            pltpu.make_async_copy(act, back_hbm, store_sems.at[2]),
        ]
        start_all(last)
        slot = len(stores) % 2
        wait_all(stores[-2])
        for third in range(3):
            some = slice(third * width // 3, (third + 1) * width // 3)
            tile_in[slot, some, :] = low(tn(att[:, some], grad_pre[...]))
        copies = []
        for side in range(2):
            o_cols = pl.ds(pl.multiple_of((core ^ side) * side_cols, 128), side_cols)
            copies += half_copies(
                me,
                tile_in.at[slot, :, o_cols],
                in_targets,
                o_sems.at[side],
                side,
                by_chips,
                (0, side_cols),
            )
        start_all(copies)
        wait_all(stores[-1])
        wait_all(copies)
        wait_all(last)

    sums = jax.ShapeDtypeStruct
    flat = sums((slots, width), jnp.bfloat16)
    packed = in_sources[0].shape[-1]
    devices = lax.axis_size("fsdp")
    if by_chips:
        line = devices // 8
        in_shapes = [sums((4, line, width // (4 * line), packed), jnp.bfloat16)] * 2
        out_shapes = [sums((4, line, hidden_cols // devices, width), jnp.bfloat16)] * 2
    else:
        in_shapes = [sums((2, width, packed), jnp.bfloat16)]
        out_shapes = [sums((hidden_cols, width), jnp.bfloat16)]
    outs = [flat, sums((slots, width), jnp.float32), flat] + in_shapes + out_shapes
    bf16, f32 = jnp.bfloat16, jnp.float32
    result = pl.pallas_call(
        kernel,
        out_shape=outs + [sums((8, width), f32)],
        in_specs=[IN_SMEM, IN_HBM, IN_HBM, IN_VMEM]
        + [IN_HBM] * (count_att + len(in_sources) + len(out_sources)),
        out_specs=[IN_HBM] * len(outs) + [IN_VMEM],
        scratch_shapes=[
            pltpu.VMEM((slots, width), bf16),
            pltpu.VMEM((slots, width), bf16),
            pltpu.VMEM((slots, width), bf16),
            pltpu.VMEM((width, width), bf16),
            pltpu.VMEM((2, width, hidden_cols // 2), bf16),
            pltpu.VMEM((hidden_cols, width), bf16),
            pltpu.VMEM((slots, width), f32),
            pltpu.VMEM((slots, width), bf16),
            pltpu.VMEM((width, slots), bf16),
            pltpu.VMEM((slots, width), f32),
            pltpu.VMEM((slots, width), f32),
            pltpu.VMEM((slots, chunk), bf16),
            pltpu.VMEM((slots, chunk), bf16),
            pltpu.VMEM((2, width, chunk), bf16),
            pltpu.VMEM((2, chunk, width), bf16),
            pltpu.SemaphoreType.DMA((2 + count_att,)),
            pltpu.SemaphoreType.DMA((2, 16)),
            pltpu.SemaphoreType.DMA((2, 16)),
            pltpu.SemaphoreType.DMA((2, 16)),
            pltpu.SemaphoreType.DMA((3,)),
            pltpu.SemaphoreType.DMA((2, 16)),
            pltpu.SemaphoreType.DMA((2, 8)),
        ],
        compiler_params=pltpu.CompilerParams(vmem_limit_bytes=60 * MIB),
        cost_estimate=cost(
            slots * width * (12 * hidden_cols + 6 * width), 60 * MIB
        ),
    )(place, tokens, cotangent, gains, *attended, *in_sources, *out_sources)
    split = 3 + len(in_shapes)
    return result[:3], result[3:split], result[split:-1], result[-1][0]


def project_back(place, tokens, gains, grad_hidden, grads, sources, by_chips):
    slots, width = tokens.shape
    side_cols = width // 2
    packed = sources[0].shape[-1]
    flat_grads = [grad for half in grads for grad in half]
    block = 256
    blocks = slots // block

    def kernel(place_ref, x_hbm, gh_hbm, gains_ref, *refs):
        refs = list(refs)

        def take(number):
            taken, refs[:] = refs[:number], refs[number:]
            return taken

        g_hbm, w_hbm = take(len(flat_grads)), take(len(sources))
        (out_hbm,) = take(1)
        targets = take(2 if by_chips else 1)
        (gain_out,) = take(1)
        x, grad, weights, parts, flipped, out, tile = take(7)
        load_sems, w_sems, tile_sems, out_sem = take(4)
        me = place_ref[0]
        core = me % 2
        gain = gains_ref[0:1, :]

        def rows_of(index):
            return pl.ds(pl.multiple_of(index * block, block), block)

        loads = [
            pltpu.make_async_copy(x_hbm, x, load_sems.at[0]),
            pltpu.make_async_copy(gh_hbm, grad, load_sems.at[1]),
        ]
        for half in range(2):
            for part in range(3):
                loads.append(
                    pltpu.make_async_copy(
                        g_hbm[3 * half + part],
                        parts.at[half, :, pl.ds(part * side_cols, side_cols)],
                        load_sems.at[2 + 3 * half + part],
                    )
                )
        w_loads = [
            column_copies(
                me, w_hbm, weights.at[side], w_sems.at[side], side, by_chips, (0, packed)
            )
            for side in range(2)
        ]
        start_all(loads)
        start_all(w_loads[0])
        start_all(w_loads[1])
        wait_all(loads)

        def flip(index, carry):
            where = rows_of(index)
            rows = wide(x[where, :])
            flipped[:, where] = low(jnp.transpose(rows * norm_scale(rows) * gain))
            return carry

        lax.fori_loop(0, blocks, flip, 0)
        copies = []
        for side in range(2):
            half = core ^ side
            for third in range(3):
                some = slice(third * width // 3, (third + 1) * width // 3)
                tile[side, some, :] = low(nn(flipped[some, :], parts[half]))
            copies.append(
                half_copies(
                    me,
                    tile.at[side],
                    targets,
                    tile_sems.at[side],
                    side,
                    by_chips,
                    (0, 3 * side_cols),
                )
            )
            start_all(copies[-1])
        wait_all(w_loads[0])
        wait_all(w_loads[1])

        def after(index, carry):
            where = rows_of(index)
            grad_normed = nt(parts[core, where, :], weights[0, :, : 3 * side_cols]) + nt(
                parts[1 - core, where, :], weights[1, :, : 3 * side_cols]
            )
            rows = wide(x[where, :])
            scale = norm_scale(rows)
            scaled = rows * scale
            out[where, :] = low(
                grad[where, :] + rms_back(scaled, scale, gain, grad_normed)
            )
            return carry + jnp.sum(grad_normed * scaled, axis=0, keepdims=True)

        gain_sum = lax.fori_loop(0, blocks, after, jnp.zeros((1, width), jnp.float32))
        gain_out[...] = jnp.broadcast_to(gain_sum, gain_out.shape)
        last = pltpu.make_async_copy(out, out_hbm, out_sem.at[0])
        last.start()
        wait_all(copies[0])
        wait_all(copies[1])
        last.wait()

    sums = jax.ShapeDtypeStruct
    if by_chips:
        line = lax.axis_size("fsdp") // 8
        shapes = [sums((4, line, width // (4 * line), 3 * side_cols), jnp.bfloat16)] * 2
    else:
        shapes = [sums((2, width, 3 * side_cols), jnp.bfloat16)]
    bf16, f32 = jnp.bfloat16, jnp.float32
    result = pl.pallas_call(
        kernel,
        out_shape=[sums((slots, width), bf16)] + shapes + [sums((8, width), f32)],
        in_specs=[IN_SMEM, IN_HBM, IN_HBM, IN_VMEM]
        + [IN_HBM] * (len(flat_grads) + len(sources)),
        out_specs=[IN_HBM] * (1 + len(shapes)) + [IN_VMEM],
        scratch_shapes=[
            pltpu.VMEM((slots, width), bf16),
            pltpu.VMEM((slots, width), f32),
            pltpu.VMEM((2, width, packed), bf16),
            pltpu.VMEM((2, slots, 3 * side_cols), bf16),
            pltpu.VMEM((width, slots), bf16),
            pltpu.VMEM((slots, width), bf16),
            pltpu.VMEM((2, width, 3 * side_cols), bf16),
            pltpu.SemaphoreType.DMA((8,)),
            pltpu.SemaphoreType.DMA((2, 16)),
            pltpu.SemaphoreType.DMA((2, 16)),
            pltpu.SemaphoreType.DMA((1,)),
        ],
        compiler_params=pltpu.CompilerParams(vmem_limit_bytes=56 * MIB),
        cost_estimate=cost(12 * slots * width * width, 30 * MIB),
    )(place, tokens, grad_hidden, gains, *flat_grads, *sources)
    return result[0], result[1:-1], result[-1][0]


def gather_by_chips(
    gain_attn, w_query, w_key, w_value, w_attn_out, gain_ffn, w_ffn_in, w_ffn_out
):
    core = lax.axis_index("fsdp") % 2
    gains = jnp.pad(jnp.stack([gain_attn, gain_ffn], 1), ((0, 0), (0, 126)))
    other_gains = swap(gains, 1)
    chip_gains = jnp.where(
        core == 0,
        jnp.concatenate([gains, other_gains], 0),
        jnp.concatenate([other_gains, gains], 0),
    )
    unit_qkv = jnp.concatenate(
        [chip_unit(w_query, core), chip_unit(w_key, core), chip_unit(w_value, core), chip_gains], 1
    )
    unit_in = jnp.concatenate([chip_unit(w_attn_out, core), chip_unit(w_ffn_in, core)], 1)
    return (
        both_cores(gather_chips(unit_qkv)),
        both_cores(gather_chips(unit_in)),
        both_cores(gather_chips(w_ffn_out)),
    )


def gather_plain(
    gain_attn, w_query, w_key, w_value, w_attn_out, gain_ffn, w_ffn_in, w_ffn_out
):
    def full(shard):
        return lax.all_gather(shard, "fsdp", axis=0, tiled=True)

    gains = jnp.pad(jnp.stack([full(gain_attn), full(gain_ffn)], 1), ((0, 0), (0, 126)))
    return (
        (halves_of(full(w_query), full(w_key), full(w_value), jnp.concatenate([gains, gains], 1)),),
        (halves_of(full(w_attn_out), full(w_ffn_in)),),
        (full(w_ffn_out),),
    )


def chip_unit(shard, core):
    half = shard.shape[1] // 2
    mine = lax.dynamic_slice_in_dim(shard, core * half, half, 1)
    other = swap(lax.dynamic_slice_in_dim(shard, (1 - core) * half, half, 1), 1)
    return jnp.where(
        core == 0, jnp.concatenate([mine, other], 0), jnp.concatenate([other, mine], 0)
    )


def owned_columns(chip_sum, core, parts):
    mine, other = own_rows(chip_sum, core)
    joined, first = [], 0
    for count in parts:
        joined.append(
            join_columns(mine[:, first : first + count], other[:, first : first + count], core)
        )
        first += count
    return joined


def per_device(
    tokens,
    lengths,
    gain_attn,
    w_query,
    w_key,
    w_value,
    w_attn_out,
    gain_ffn,
    w_ffn_in,
    w_ffn_out,
    bucket_bias_matrix,
    cotangent,
):
    slot_count, width = tokens.shape
    heads = bucket_bias_matrix.shape[1]
    devices = lax.axis_size("fsdp")
    valid = jnp.sum(lengths, axis=-1)
    factor = 1.0 / math.sqrt(slot_count * devices)
    me = lax.axis_index("fsdp")
    core = me % 2
    place = me.astype(jnp.int32)[None]
    side = width // 2
    by_chips = devices == 32
    in_qkv, in_ffn, in_out = (gather_by_chips if by_chips else gather_plain)(
        gain_attn, w_query, w_key, w_value, w_attn_out, gain_ffn, w_ffn_in, w_ffn_out
    )
    planes = bias_planes(bucket_bias_matrix)
    query, key, value, gains = project_qkv(place, tokens, in_qkv, by_chips)
    pairs = heads // 2
    first_half = attend(valid, query, key, value, planes, 0, pairs // 2)
    second_half = attend(valid, query, key, value, planes, pairs // 2, pairs // 2)
    attended, probs = zip(first_half, second_half)
    (output, grad_hidden, grad_attended), part_in, part_out, gain_ffn_sum = feed_forward(
        place, tokens, attended, cotangent, gains, in_ffn, in_out, by_chips
    )
    backs = [
        attend_back(
            query, key, value, grad_attended, probs[half], half * pairs // 2, pairs // 2, heads
        )
        for half in range(2)
    ]
    diagonals = jnp.concatenate([back[3].reshape(heads // 2, 16 * SEQ) for back in backs])
    grad_tokens, part_qkv, gain_attn_sum = project_back(
        place, tokens, gains, grad_hidden, [back[:3] for back in backs], in_qkv, by_chips
    )
    onehot = (line_ids().reshape(-1)[:, None] == np.arange(NB)[None, :]).astype(np.float32)
    table = lax.dot_general(
        jnp.asarray(onehot),
        diagonals,
        (((0,), (1,)), ((), ())),
        precision=lax.Precision.HIGHEST,
    )
    if by_chips:
        sum_out = scatter_chips(part_out[1], part_out[0])
        sum_o, sum_in = owned_columns(
            scatter_chips(part_in[1], part_in[0]), core, (side, part_in[0].shape[-1] - side)
        )
        sum_q, sum_k, sum_v = owned_columns(
            scatter_chips(part_qkv[1], part_qkv[0]), core, (side, side, side)
        )
        sums = [sum_q, sum_k, sum_v, sum_o, sum_in, sum_out]
    else:
        sums = sum_plain(
            jnp.concatenate([part_qkv[0], part_in[0][:, :, :side]], 2),
            part_in[0][:, :, side:],
            part_out[0],
        )
    sums = [total * factor for total in sums]
    small = sum_everywhere(
        jnp.concatenate([gain_attn_sum, gain_ffn_sum, table.reshape(-1)]).reshape(-1, 128)
    )
    small = small.reshape(-1) * factor
    shard = gain_attn.shape[0]
    return (
        output,
        grad_tokens,
        lax.dynamic_slice_in_dim(small, me * shard, shard),
        sums[0],
        sums[1],
        sums[2],
        sums[3],
        lax.dynamic_slice_in_dim(small, width + me * shard, shard),
        sums[4],
        sums[5],
        small[2 * width :].reshape(bucket_bias_matrix.shape),
    )


def solution(mesh):
    placed = (
        P("fsdp", None),
        P("fsdp", None),
        P("fsdp"),
        P("fsdp", None),
        P("fsdp", None),
        P("fsdp", None),
        P("fsdp", None),
        P("fsdp"),
        P("fsdp", None),
        P("fsdp", None),
        P(),
        P("fsdp", None),
    )
    return jax.shard_map(
        per_device,
        mesh=mesh,
        in_specs=placed,
        out_specs=(
            P("fsdp", None),
            P("fsdp", None),
            P("fsdp"),
            P("fsdp", None),
            P("fsdp", None),
            P("fsdp", None),
            P("fsdp", None),
            P("fsdp"),
            P("fsdp", None),
            P("fsdp", None),
            P(),
        ),
        check_vma=False,
    )
```

time: 1150 us -> 408 us (0.35)
  waiting for transfers between devices: 655 us -> 123 us
  matrix products: 192 us -> 1.75 us
  Pallas kernels: 0 us -> 157 us
  local copies, waits for them, and re-layouts: 165 us -> 37.6 us
  blocking collectives: 81.9 us -> 0 us
  starting transfers between devices: 0.47 us -> 69.1 us
  other arithmetic: 27.6 us -> 13.6 us
  between operations: 15 us -> 1.88 us
    reduce_scatter x6 -> x0, waiting for transfers between devices: 477 us -> none  [the longest x1 140 us: per_device(): lax.psum_scatter(grad_ffn_in, 'fsdp', scatter_dimension=0, tiled=True)]
    dot_general x35 -> x2, matrix products: 192 us -> 1.75 us  [the longest x1 1.58 us: per_device(): lax.dot_general(jnp.asarray(onehot), diagonals, (((0,), (1,)), ((), ())),...]
    all_gather x6 -> x0, waiting for transfers between devices: 175 us -> none  [the longest x1 59.9 us: per_device(): lax.all_gather(w_ffn_in, 'fsdp', axis=0, tiled=True)]
    pallas_call x0 -> x8, Pallas kernels: none -> 157 us  [the longest x1 52.1 us: feed_forward(): pl.pallas_call(kernel, out_shape=outs + [sums((8, width), f32)], in_specs...]
    ppermute x0 -> x79, waiting for transfers between devices: none -> 123 us  [swap(): return lax.ppermute(array, 'fsdp', flip(mask, lax.axis_size('fsdp')))]
    unnamed x2 -> x0, blocking collectives: 81.9 us -> none
    ppermute x0 -> x79, starting transfers between devices: none -> 69.1 us  [swap(): return lax.ppermute(array, 'fsdp', flip(mask, lax.axis_size('fsdp')))]
    while x44 -> x0, local copies, waits for them, and re-layouts: 68.4 us -> none
  transfers between devices with their start and end apart: 12 -> 79, of which waited for: 9 -> 30; matrix products, arithmetic and copies ran while one was open for 29% -> 6% of each run, Pallas kernels for 0% -> 12%
where the time goes in v3:
time: 408 us; the launch traced here: 404 us
  Pallas kernels  157 us (38%)
  waiting for transfers between devices  123 us (30%)
  starting transfers between devices  69.1 us (17%)
  local copies, waits for them, and re-layouts  37.6 us (9%)
  other arithmetic  13.6 us (3%)
    ppermute x79, waiting for transfers between devices, swap(): return lax.ppermute(array, 'fsdp', flip(mask, lax.axis_size('fsdp')))  123 us
    ppermute x79, starting transfers between devices, swap(): return lax.ppermute(array, 'fsdp', flip(mask, lax.axis_size('fsdp')))  69.1 us
    pallas_call x1, Pallas kernels, feed_forward(): pl.pallas_call(kernel, out_shape=outs + [sums((8, width), f32)], in_specs...  52.1 us
    pallas_call x2, Pallas kernels, attend_back(): pl.pallas_call(kernel, grid=(count, seqs), in_specs=[block, block, block,...  36.7 us
    pallas_call x2, Pallas kernels, attend(): pl.pallas_call(kernel, grid_spec=pltpu.PrefetchScalarGridSpec(num_scalar_...  32 us
    unnamed x123, local copies, waits for them, and re-layouts  26.5 us
    pallas_call x1, Pallas kernels, project_back(): pl.pallas_call(kernel, out_shape=[sums((slots, width), bf16)] + shapes +...  19.5 us
    pallas_call x1, Pallas kernels, project_qkv(): pl.pallas_call(kernel, grid_spec=pltpu.PrefetchScalarGridSpec(num_scalar_...  14.1 us
  transfers between devices with their start and end apart: 79, of which 30 were waited for; matrix products, arithmetic and copies ran while one was open for 6% of the time, Pallas kernels for 12%

profile of v3, /device:TPU:0, one launch (start us, length us, event | category | flops | bytes accessed | tf_op | source)
XLA Modules:
  0.0 403.7 jit_solution(8530691598223068835)
XLA Ops:
  0.7 3.1 collective-permute-start.30
  14.1 3.5 collective-permute-start.6
  20.6 8.5 %collective-permute-done.5 = bf16[48,1280]{1,0:T(8,128)(2,1)S(1)} collective-permute-done((bf16[48,1280]{1,0:T(8,128)(2,1)S(1)}, bf16[48,1280]{1,0:T(8,128)(2,1)S(1)}, u32[]{:S(2)}, u32[]{:S(2)}) %collective-permute-start.5) | collective-permute-done | bytes 122912 | tf_op jit(solution)/shard_map/ppermute | solution.py:39
  30.9 3.1 collective-permute-start.19
  38.2 9.3 %collective-permute-done.19 = bf16[48,1920]{1,0:T(8,128)(2,1)S(1)} collective-permute-done((bf16[48,1920]{1,0:T(8,128)(2,1)S(1)}, bf16[48,1920]{1,0:T(8,128)(2,1)S(1)}, u32[]{:S(2)}, u32[]{:S(2)}) %collective-permute-start.19) | collective-permute-done | bytes 184352 | tf_op jit(solution)/shard_map/ppermute | solution.py:39
  52.0 11.9 %collective-permute-done.34.refs_14_ = bf16[4,96,768]{2,1,0:T(8,128)(2,1)} collective-permute-done((bf16[4,96,768]{2,1,0:T(8,128)(2,1)S(1)}, bf16[4,96,768]{2,1,0:T(8,128)(2,1)}, u32[]{:S(2)}, u32[]{:S(2)}) %collective-permute-start.34) | collective-permute-done | bytes 589856 | tf_op jit(solution)/shard_map/ppermute | solution.py:39
  68.4 16.8 %collective-permute-done.9.refs_3_.refs_9_ = bf16[2,48,1280]{2,1,0:T(8,128)(2,1)S(1)} collective-permute-done((bf16[2,48,1280]{2,1,0:T(8,128)(2,1)S(1)}, bf16[2,48,1280]{2,1,0:T(8,128)(2,1)S(1)}, u32[]{:S(2)}, u32[]{:S(2)}) %collective-permute-start.9) | collective-permute-done | bytes 245792 | tf_op jit(solution)/shard_map/ppermute | solution.py:39
  89.5 4.3 %collective-permute-done.35.refs_15_ = bf16[2,96,768]{2,1,0:T(8,128)(2,1)S(1)} collective-permute-done((bf16[2,96,768]{2,1,0:T(8,128)(2,1)S(1)}, bf16[2,96,768]{2,1,0:T(8,128)(2,1)S(1)}, u32[]{:S(2)}, u32[]{:S(2)}) %collective-permute-start.35) | collective-permute-done | bytes 294944 | tf_op jit(solution)/shard_map/ppermute | solution.py:39
  112.3 14.1 %shard_map.221 = (bf16[1024,768]{1,0:T(8,128)(2,1)S(1)}, bf16[1024,768]{1,0:T(8,128)(2,1)S(1)}, bf16[1024,768]{1,0:T(8,128)(2,1)S(1)}, f32[8,768]{1,0:T(8,128)S(1)}) custom-call(s32[1]{0:T(128)} %bitcast.place_ref, bf16[1024,768]{1,0:T(8,128)(2,1)S(1)} %copy-done.6, bf16[4,48,1280]{2,1,0:T(8,128)(2,1)S(1)} %pad_maximum_fusion.2.refs_0_.refs_6_, ...), custom_call_target="tpu_custom_call" | custom-call | flops 3623878656 | bytes 9437184 | tf_op jit(solution)/shard_map/pallas_call | solution.py:367
  127.7 16.2 %shard_map.224 = (bf16[1024,384]{1,0:T(8,128)(2,1)S(1)}, bf16[2,6,512,512]{3,2,1,0:T(8,128)(2,1)S(1)}) custom-call(s32[2]{0:T(128)S(1)} %reduce_sum.9.valid_ref, bf16[1024,768]{1,0:T(8,128)(2,1)S(1)} %get-tuple-element.40.q_ref, bf16[1024,768]{1,0:T(8,128)(2,1)S(1)} %get-tuple-element.41.k_ref, bf16[1024,768]{1,0:T(8,128)(2,1)S(1)} %get-tuple-element.42.v_ref, ...), custom_call_target="tpu_custom_call" | custom-call | flops 3221225472 | bytes 12582912 | tf_op jit(solution)/shard_map/pallas_call | solution.py:424
  147.4 15.8 %shard_map.223 = (bf16[1024,384]{1,0:T(8,128)(2,1)S(1)}, bf16[2,6,512,512]{3,2,1,0:T(8,128)(2,1)S(1)}) custom-call(s32[2]{0:T(128)S(1)} %reduce_sum.9.valid_ref, bf16[1024,768]{1,0:T(8,128)(2,1)S(1)} %get-tuple-element.40.q_ref, bf16[1024,768]{1,0:T(8,128)(2,1)S(1)} %get-tuple-element.41.k_ref, bf16[1024,768]{1,0:T(8,128)(2,1)S(1)} %get-tuple-element.42.v_ref, ...), custom_call_target="tpu_custom_call" | custom-call | flops 3221225472 | bytes 12582912 | tf_op jit(solution)/shard_map/pallas_call | solution.py:424
  168.3 52.1 %shard_map.225 = (bf16[1024,768]{1,0:T(8,128)(2,1)}, f32[1024,768]{1,0:T(8,128)}, bf16[1024,768]{1,0:T(8,128)(2,1)}, bf16[4,4,48,1920]{3,2,1,0:T(8,128)(2,1)}, b...) custom-call(s32[1]{0:T(128)} %bitcast.place_ref, ...), custom_call_target="tpu_custom_call" | custom-call | flops 32614907904 | bytes 62914560 | tf_op jit(solution)/shard_map/pallas_call | solution.py:743
  223.2 18.2 %shard_map.227 = (bf16[1024,384]{1,0:T(8,128)(2,1)S(1)}, bf16[1024,384]{1,0:T(8,128)(2,1)S(1)}, bf16[1024,384]{1,0:T(8,128)(2,1)S(1)}, f32[3,2,8,1024]{3,2,1,0:T(8,128)S(1)}) custom-call(bf16[1024,768]{1,0:T(8,128)(2,1)S(1)} %copy-done.21, bf16[1024,768]{1,0:T(8,128)(2,1)S(1)} %copy-done.23, bf16[1024,768]{1,0:T(8,128)(2,1)S(1)} %copy-done.25, ...), custom_call_target="tpu_custom_call" | custom-call | flops 6442450944 | bytes 12582912 | tf_op jit(solution)/shard_map/pallas_call | solution.py:529
  241.5 18.5 %shard_map.226 = (bf16[1024,384]{1,0:T(8,128)(2,1)S(1)}, bf16[1024,384]{1,0:T(8,128)(2,1)S(1)}, bf16[1024,384]{1,0:T(8,128)(2,1)S(1)}, f32[3,2,8,1024]{3,2,1,0:T(8,128)S(1)}) custom-call(bf16[1024,768]{1,0:T(8,128)(2,1)S(1)} %copy-done.21, bf16[1024,768]{1,0:T(8,128)(2,1)S(1)} %copy-done.23, bf16[1024,768]{1,0:T(8,128)(2,1)S(1)} %copy-done.26, ...), custom_call_target="tpu_custom_call" | custom-call | flops 6442450944 | bytes 12582912 | tf_op jit(solution)/shard_map/pallas_call | solution.py:529
  262.8 19.5 %shard_map.228 = (bf16[1024,768]{1,0:T(8,128)(2,1)}, bf16[4,4,48,1152]{3,2,1,0:T(8,128)(2,1)}, bf16[4,4,48,1152]{3,2,1,0:T(8,128)(2,1)}, f32[8,768]{1,0:T(8,128)}) custom-call(s32[1]{0:T(128)} %bitcast.place_ref, bf16[1024,768]{1,0:T(8,128)(2,1)} %x_hbm.3, f32[1024,768]{1,0:T(8,128)} %get-tuple-element.46.gh_hbm, f32[8,768]{1,0:T(8,128)} %copy-done.36, ...), custom_call_target="tpu_custom_call" | custom-call | flops 7247757312 | bytes 31457280 | tf_op jit(solution)/shard_map/pallas_call | solution.py:890
  313.3 3.4 collective-permute-done.50
  323.5 3.9 collective-permute-start.55
  341.8 5.8 %collective-permute-done.72 = bf16[2,96,768]{2,1,0:T(8,128)(2,1)S(1)} collective-permute-done((bf16[2,96,768]{2,1,0:T(8,128)(2,1)S(1)}, bf16[2,96,768]{2,1,0:T(8,128)(2,1)S(1)}, u32[]{:S(2)}, u32[]{:S(2)}) %collective-permute-start.72) | collective-permute-done | bytes 294944 | tf_op jit(solution)/shard_map/ppermute | solution.py:39
  353.5 5.4 %collective-permute-done.75 = bf16[2,96,768]{2,1,0:T(8,128)(2,1)S(1)} collective-permute-done((bf16[2,96,768]{2,1,0:T(8,128)(2,1)S(1)}, bf16[2,96,768]{2,1,0:T(8,128)(2,1)S(1)}, u32[]{:S(2)}, u32[]{:S(2)}) %collective-permute-start.75) | collective-permute-done | bytes 294944 | tf_op jit(solution)/shard_map/ppermute | solution.py:39
  359.4 6.3 %collective-permute-done.59 = bf16[2,48,1920]{2,1,0:T(8,128)(2,1)S(1)} collective-permute-done((bf16[2,48,1920]{2,1,0:T(8,128)(2,1)S(1)}, bf16[2,48,1920]{2,1,0:T(8,128)(2,1)S(1)}, u32[]{:S(2)}, u32[]{:S(2)}) %collective-permute-start.59) | collective-permute-done | bytes 368672 | tf_op jit(solution)/shard_map/ppermute | solution.py:39
  365.7 3.5 collective-permute-done.61
  373.3 3.8 collective-permute-done.64
  383.3 10.8 %collective-permute-done.66 = bf16[48,1920]{1,0:T(8,128)(2,1)S(1)} collective-permute-done((bf16[48,1920]{1,0:T(8,128)(2,1)S(1)}, bf16[48,1920]{1,0:T(8,128)(2,1)S(1)}, u32[]{:S(2)}, u32[]{:S(2)}) %collective-permute-start.66) | collective-permute-done | bytes 184352 | tf_op jit(solution)/shard_map/ppermute | solution.py:39
  394.3 6.9 %collective-permute-done.77 = bf16[96,768]{1,0:T(8,128)(2,1)S(1)} collective-permute-done((bf16[96,768]{1,0:T(8,128)(2,1)S(1)}, bf16[96,768]{1,0:T(8,128)(2,1)S(1)}, u32[]{:S(2)}, u32[]{:S(2)}) %collective-permute-start.77) | collective-permute-done | bytes 147488 | tf_op jit(solution)/shard_map/ppermute | solution.py:39
  (341 shorter events, 137.1 us)
Async XLA Ops:
  0.7 33.3 %collective-permute-start.30 = (bf16[96,768]{1,0:T(8,128)(2,1)}, bf16[96,768]{1,0:T(8,128)(2,1)S(1)}, u32[]{:S(2)}, u32[]{:S(2)}) collective-permute-start(bf16[96,768]{1,0:T(8,128)(2,1)} %param.23), channel_id=1, source_target_pairs={{0,8},{1,9},{2,10},{3,11},{4,12},{5,13},{6,14},{7,15},{8,0},{9,1},... | collective-permute-start | bytes 442376 | tf_op jit(solution)/shard_map/ppermute | solution.py:39
  3.8 32.7 %collective-permute-start.31 = (bf16[96,768]{1,0:T(8,128)(2,1)}, bf16[96,768]{1,0:T(8,128)(2,1)S(1)}, u32[]{:S(2)}, u32[]{:S(2)}) collective-permute-start(bf16[96,768]{1,0:T(8,128)(2,1)} %param.23), channel_id=1, source_target_pairs={{0,16},{1,17},{2,18},{3,19},{4,20},{5,21},{6,22},{7,23},{8,24},{9,... | collective-permute-start | bytes 442376 | tf_op jit(solution)/shard_map/ppermute | solution.py:39
  29.3 20.7 %collective-permute-start.8 = (bf16[4,48,1280]{2,1,0:T(8,128)(2,1)S(1)}, bf16[4,48,1280]{2,1,0:T(8,128)(2,1)S(1)}, u32[]{:S(2)}, u32[]{:S(2)}) collective-permute-start(bf16[4,48,1280]{2,1,0:T(8,128)(2,1)S(1)} %pad_maximum_fusion.2.refs_0_.refs_6_), channel_id=1, source_target_pairs={{0,4},{1,5},{2,6},{3,7},{4,0},{5,1},{6,2},{7,3},{8,12},{9,13},{10,... | collective-permute-start | bytes 1474568 | tf_op jit(solution)/shard_map/ppermute | solution.py:39
  50.2 38.6 %collective-permute-start.22 = (bf16[4,48,1920]{2,1,0:T(8,128)(2,1)S(1)}, bf16[4,48,1920]{2,1,0:T(8,128)(2,1)S(1)}, u32[]{:S(2)}, u32[]{:S(2)}) collective-permute-start(bf16[4,48,1920]{2,1,0:T(8,128)(2,1)S(1)} %pad_maximum_fusion.refs_2_), channel_id=1, source_target_pairs={{0,4},{1,5},{2,6},{3,7},{4,0},{5,1},{6,2},{7,3},{8,12},{9,13},{10,... | collective-permute-start | bytes 2211848 | tf_op jit(solution)/shard_map/ppermute | solution.py:39
  51.4 37.4 %collective-permute-start.21 = (bf16[4,48,1920]{2,1,0:T(8,128)(2,1)S(1)}, bf16[4,48,1920]{2,1,0:T(8,128)(2,1)S(1)}, u32[]{:S(2)}, u32[]{:S(2)}) collective-permute-start(bf16[4,48,1920]{2,1,0:T(8,128)(2,1)S(1)} %pad_maximum_fusion.refs_2_), channel_id=1, source_target_pairs={{0,2},{1,3},{2,0},{3,1},{4,6},{5,7},{6,4},{7,5},{8,10},{9,11},{10,... | collective-permute-start | bytes 2211848 | tf_op jit(solution)/shard_map/ppermute | solution.py:39
  63.8 25.6 %collective-permute-start.25 = (bf16[4,48,1920]{2,1,0:T(8,128)(2,1)S(1)}, bf16[4,48,1920]{2,1,0:T(8,128)(2,1)S(1)}, u32[]{:S(2)}, u32[]{:S(2)}) collective-permute-start(bf16[4,48,1920]{2,1,0:T(8,128)(2,1)S(1)} %pad_maximum_fusion.refs_2_), channel_id=1, source_target_pairs={{0,1},{1,0},{2,3},{3,2},{4,5},{5,4},{6,7},{7,6},{8,9},{9,8},{10,11... | collective-permute-start | bytes 2211848 | tf_op jit(solution)/shard_map/ppermute | solution.py:39
  64.7 20.5 %collective-permute-start.9 = (bf16[2,48,1280]{2,1,0:T(8,128)(2,1)S(1)}, bf16[2,48,1280]{2,1,0:T(8,128)(2,1)S(1)}, u32[]{:S(2)}, u32[]{:S(2)}) collective-permute-start(bf16[2,48,1280]{2,1,0:T(8,128)(2,1)S(1)} %slice.225), channel_id=1, source_target_pairs={{0,2},{1,3},{2,0},{3,1},{4,6},{5,7},{6,4},{7,5},{8,10},{9,11},{10,... | collective-permute-start | bytes 737288 | tf_op jit(solution)/shard_map/ppermute | solution.py:39
  66.2 21.4 %collective-permute-start.10 = (bf16[2,48,1280]{2,1,0:T(8,128)(2,1)S(1)}, bf16[2,48,1280]{2,1,0:T(8,128)(2,1)S(1)}, u32[]{:S(2)}, u32[]{:S(2)}) collective-permute-start(bf16[2,48,1280]{2,1,0:T(8,128)(2,1)S(1)} %slice.226), channel_id=1, source_target_pairs={{0,4},{1,5},{2,6},{3,7},{4,0},{5,1},{6,2},{7,3},{8,12},{9,13},{10,... | collective-permute-start | bytes 737288 | tf_op jit(solution)/shard_map/ppermute | solution.py:39
  88.9 18.0 %collective-permute-start.38 = (bf16[4,96,768]{2,1,0:T(8,128)(2,1)}, bf16[4,96,768]{2,1,0:T(8,128)(2,1)}, u32[]{:S(2)}, u32[]{:S(2)}) collective-permute-start(bf16[4,96,768]{2,1,0:T(8,128)(2,1)} %collective-permute-done.33.refs_13_), channel_id=1, source_target_pairs={{0,1},{1,0},{2,3},{3,2},{4,5},{5,4},{6,7},{7,6},{8,9},{9,8},{10,11... | collective-permute-start | bytes 1769480 | tf_op jit(solution)/shard_map/ppermute | solution.py:39
  96.7 30.3 %collective-permute-start.39 = (bf16[4,96,768]{2,1,0:T(8,128)(2,1)}, bf16[4,96,768]{2,1,0:T(8,128)(2,1)}, u32[]{:S(2)}, u32[]{:S(2)}) collective-permute-start(bf16[4,96,768]{2,1,0:T(8,128)(2,1)} %collective-permute-done.34.refs_14_), channel_id=1, source_target_pairs={{0,1},{1,0},{2,3},{3,2},{4,5},{5,4},{6,7},{7,6},{8,9},{9,8},{10,11... | collective-permute-start | bytes 1769480 | tf_op jit(solution)/shard_map/ppermute | solution.py:39
  99.0 28.1 %collective-permute-start.23 = (bf16[2,48,1920]{2,1,0:T(8,128)(2,1)}, bf16[2,48,1920]{2,1,0:T(8,128)(2,1)}, u32[]{:S(2)}, u32[]{:S(2)}) collective-permute-start(bf16[2,48,1920]{2,1,0:T(8,128)(2,1)} %slice.227), channel_id=1, source_target_pairs={{0,2},{1,3},{2,0},{3,1},{4,6},{5,7},{6,4},{7,5},{8,10},{9,11},{10,... | collective-permute-start | bytes 1105928 | tf_op jit(solution)/shard_map/ppermute | solution.py:39
  100.3 27.3 %collective-permute-start.24 = (bf16[2,48,1920]{2,1,0:T(8,128)(2,1)}, bf16[2,48,1920]{2,1,0:T(8,128)(2,1)}, u32[]{:S(2)}, u32[]{:S(2)}) collective-permute-start(bf16[2,48,1920]{2,1,0:T(8,128)(2,1)} %slice.228), channel_id=1, source_target_pairs={{0,4},{1,5},{2,6},{3,7},{4,0},{5,1},{6,2},{7,3},{8,12},{9,13},{10,... | collective-permute-start | bytes 1105928 | tf_op jit(solution)/shard_map/ppermute | solution.py:39
  106.8 60.0 %collective-permute-start.26 = (bf16[4,48,1920]{2,1,0:T(8,128)(2,1)}, bf16[4,48,1920]{2,1,0:T(8,128)(2,1)S(1)}, u32[]{:S(2)}, u32[]{:S(2)}) collective-permute-start(bf16[4,48,1920]{2,1,0:T(8,128)(2,1)} %copy-done.44), channel_id=1, source_target_pairs={{0,1},{1,0},{2,3},{3,2},{4,5},{5,4},{6,7},{7,6},{8,9},{9,8},{10,11... | collective-permute-start | bytes 2211848 | tf_op jit(solution)/shard_map/ppermute | solution.py:39
  106.9 59.9 %collective-permute-start.27 = (bf16[4,48,1920]{2,1,0:T(8,128)(2,1)}, bf16[4,48,1920]{2,1,0:T(8,128)(2,1)S(1)}, u32[]{:S(2)}, u32[]{:S(2)}) collective-permute-start(bf16[4,48,1920]{2,1,0:T(8,128)(2,1)} %copy-done.43), channel_id=1, source_target_pairs={{0,1},{1,0},{2,3},{3,2},{4,5},{5,4},{6,7},{7,6},{8,9},{9,8},{10,11... | collective-permute-start | bytes 2211848 | tf_op jit(solution)/shard_map/ppermute | solution.py:39
  127.0 19.6 %collective-permute-start.40 = (bf16[2,96,768]{2,1,0:T(8,128)(2,1)S(1)}, bf16[2,96,768]{2,1,0:T(8,128)(2,1)S(1)}, u32[]{:S(2)}, u32[]{:S(2)}) collective-permute-start(bf16[2,96,768]{2,1,0:T(8,128)(2,1)S(1)} %copy-done.55), channel_id=1, source_target_pairs={{0,1},{1,0},{2,3},{3,2},{4,5},{5,4},{6,7},{7,6},{8,9},{9,8},{10,11... | collective-permute-start | bytes 884744 | tf_op jit(solution)/shard_map/ppermute | solution.py:39
  127.2 39.6 %collective-permute-start.28 = (bf16[2,48,1920]{2,1,0:T(8,128)(2,1)}, bf16[2,48,1920]{2,1,0:T(8,128)(2,1)S(1)}, u32[]{:S(2)}, u32[]{:S(2)}) collective-permute-start(bf16[2,48,1920]{2,1,0:T(8,128)(2,1)} %collective-permute-done.23.refs_5_), channel_id=1, source_target_pairs={{0,1},{1,0},{2,3},{3,2},{4,5},{5,4},{6,7},{7,6},{8,9},{9,8},{10,11... | collective-permute-start | bytes 1105928 | tf_op jit(solution)/shard_map/ppermute | solution.py:39
  127.6 39.2 %collective-permute-start.29 = (bf16[2,48,1920]{2,1,0:T(8,128)(2,1)}, bf16[2,48,1920]{2,1,0:T(8,128)(2,1)S(1)}, u32[]{:S(2)}, u32[]{:S(2)}) collective-permute-start(bf16[2,48,1920]{2,1,0:T(8,128)(2,1)} %collective-permute-done.24.refs_6_), channel_id=1, source_target_pairs={{0,1},{1,0},{2,3},{3,2},{4,5},{5,4},{6,7},{7,6},{8,9},{9,8},{10,11... | collective-permute-start | bytes 1105928 | tf_op jit(solution)/shard_map/ppermute | solution.py:39
  147.4 19.4 %collective-permute-start.41 = (bf16[2,96,768]{2,1,0:T(8,128)(2,1)S(1)}, bf16[2,96,768]{2,1,0:T(8,128)(2,1)S(1)}, u32[]{:S(2)}, u32[]{:S(2)}) collective-permute-start(bf16[2,96,768]{2,1,0:T(8,128)(2,1)S(1)} %copy-done.57), channel_id=1, source_target_pairs={{0,1},{1,0},{2,3},{3,2},{4,5},{5,4},{6,7},{7,6},{8,9},{9,8},{10,11... | collective-permute-start | bytes 884744 | tf_op jit(solution)/shard_map/ppermute | solution.py:39
  287.1 32.0 %collective-permute-start.69 = (bf16[4,4,96,768]{3,2,1,0:T(8,128)(2,1)}, bf16[4,4,96,768]{3,2,1,0:T(8,128)(2,1)}, u32[]{:S(2)}, u32[]{:S(2)}) collective-permute-start(bf16[4,4,96,768]{3,2,1,0:T(8,128)(2,1)} %get-tuple-element.66), channel_id=1, source_target_pairs={{0,1},{1,0},{2,3},{3,2},{4,5},{5,4},{6,7},{7,6},{8,9},{9,8},{10,11... | collective-permute-start | bytes 7077896 | tf_op jit(solution)/shard_map/ppermute | solution.py:39
  300.3 38.1 %collective-permute-start.58 = (bf16[4,4,48,1920]{3,2,1,0:T(8,128)(2,1)}, bf16[4,4,48,1920]{3,2,1,0:T(8,128)(2,1)}, u32[]{:S(2)}, u32[]{:S(2)}) collective-permute-start(bf16[4,4,48,1920]{3,2,1,0:T(8,128)(2,1)} %get-tuple-element.64), channel_id=1, source_target_pairs={{0,1},{1,0},{2,3},{3,2},{4,5},{5,4},{6,7},{7,6},{8,9},{9,8},{10,11... | collective-permute-start | bytes 8847368 | tf_op jit(solution)/shard_map/ppermute | solution.py:39
  334.0 19.2 %collective-permute-start.76 = (bf16[2,96,768]{2,1,0:T(8,128)(2,1)S(1)}, bf16[2,96,768]{2,1,0:T(8,128)(2,1)S(1)}, u32[]{:S(2)}, u32[]{:S(2)}) collective-permute-start(bf16[2,96,768]{2,1,0:T(8,128)(2,1)S(1)} %get-tuple-element.109), channel_id=1, source_target_pairs={{0,4},{1,5},{2,6},{3,7},{4,0},{5,1},{6,2},{7,3},{8,12},{9,13},{10,... | collective-permute-start | bytes 884744 | tf_op jit(solution)/shard_map/ppermute | solution.py:39
  353.1 41.2 %collective-permute-start.73 = (bf16[96,768]{1,0:T(8,128)(2,1)S(1)}, bf16[96,768]{1,0:T(8,128)(2,1)S(1)}, u32[]{:S(2)}, u32[]{:S(2)}) collective-permute-start(bf16[96,768]{1,0:T(8,128)(2,1)S(1)} %slice_bitcast_fusion.30), channel_id=1, source_target_pairs={{0,8},{1,9},{2,10},{3,11},{4,12},{5,13},{6,14},{7,15},{8,0},{9,1},... | collective-permute-start | bytes 442376 | tf_op jit(solution)/shard_map/ppermute | solution.py:39
  379.6 21.6 %collective-permute-start.77 = (bf16[96,768]{1,0:T(8,128)(2,1)S(1)}, bf16[96,768]{1,0:T(8,128)(2,1)S(1)}, u32[]{:S(2)}, u32[]{:S(2)}) collective-permute-start(bf16[96,768]{1,0:T(8,128)(2,1)S(1)} %get-tuple-element.120), channel_id=1, source_target_pairs={{0,16},{1,17},{2,18},{3,19},{4,20},{5,21},{6,22},{7,23},{8,24},{9,... | collective-permute-start | bytes 442376 | tf_op jit(solution)/shard_map/ppermute | solution.py:39
  381.6 19.6 %collective-permute-start.78 = (bf16[96,768]{1,0:T(8,128)(2,1)S(1)}, bf16[96,768]{1,0:T(8,128)(2,1)S(1)}, u32[]{:S(2)}, u32[]{:S(2)}) collective-permute-start(bf16[96,768]{1,0:T(8,128)(2,1)S(1)} %get-tuple-element.121), channel_id=1, source_target_pairs={{0,24},{1,25},{2,26},{3,27},{4,28},{5,29},{6,30},{7,31},{8,16},{9,... | collective-permute-start | bytes 442376 | tf_op jit(solution)/shard_map/ppermute | solution.py:39
  (115 other events, 1590.1 us)
